TPU v7x, 512 devices: a whole 4x8x8 slice. The times are simulated.
512 devices in a mesh: dp: 128 (over z, x, y_hi, core), layer: 4 (over y_lo).
Axes of the slice: x: 4, y: 8 (y_hi: 2, y_lo: 4; y = y_hi * 4 + y_lo), z: 8, core: 2. Of those that a mesh axis runs over, the one named last changes fastest.
Arguments:
- activations: bfloat16 [4, 16384, 9728], P('layer', 'dp'), may hold values from -0.796875 to 1.1953125
- out_grads: bfloat16 [4, 16384, 3584], P('layer', 'dp'), may hold values from -0.796875 to 1.1953125
- in_basis: bfloat16 [4, 9728, 64], P('layer', 'dp'), may hold values from -0.0625 to 0.0625
- out_basis: bfloat16 [4, 3584, 64], P('layer', 'dp'), may hold values from -0.09375 to 0.09375
- queries: bfloat16 [4, 64, 4096], P('layer'), may hold values from -6 to 6
- pair_lengths: int32 [128, 4], P('dp'), may hold values from 1 to 32, 96 in all within a row
- query_index: int32 [512, 8], P('dp'), may hold values from 0 to 63
Outputs:
- sketches: bfloat16 [4, 512, 4096], P('layer', 'dp')
- scores: float32 [512, 8], P('dp')
Inputs may be any that keep to these rules, and one draw needn't show every extreme that they name: `pair_lengths`: the lengths in one row sum to 96, and one of them is 32.
All inputs are finite; a program needn't handle non-finite values.
Results may differ from a plain program's by a relative error of at most 0.0062.
Values may be sent and summed in bfloat16 or wider, within the bound.
A program may use at most 64 MiB of HBM per device.

v0:
```python
import jax
import jax.numpy as jnp
from jax import lax
from jax.sharding import PartitionSpec as P

damp_ratio = 0.5


def local(activations, out_grads, in_basis, out_basis, queries, pair_lengths, query_index):
    hidden_acts = activations[0]
    grads_local = out_grads[0]
    token_rows = hidden_acts.shape[0]
    pairs_local = pair_lengths.shape[1]
    slot_len = token_rows // pairs_local
    in_rank = in_basis.shape[2]
    out_rank = out_basis.shape[2]
    columns = hidden_acts
    right_full = jnp.dot(
        columns,
        lax.all_gather(in_basis, "dp", axis=1, tiled=True)[0],
        preferred_element_type=jnp.float32,
    )
    columns = grads_local
    left_full = jnp.dot(
        columns,
        lax.all_gather(out_basis, "dp", axis=1, tiled=True)[0],
        preferred_element_type=jnp.float32,
    )
    positions = jnp.arange(slot_len, dtype=jnp.int32)
    token_mask = (
        (positions[None, :] < pair_lengths[0][:, None]).astype(jnp.float32).reshape(token_rows, 1)
    )
    right_proj = right_full.astype(jnp.bfloat16)
    left_proj = (token_mask * left_full).astype(jnp.bfloat16)
    sketch = jnp.einsum(
        "ptk,ptj->pkj",
        left_proj.reshape(pairs_local, slot_len, out_rank),
        right_proj.reshape(pairs_local, slot_len, in_rank),
        preferred_element_type=jnp.float32,
    )
    sketch = sketch.reshape(pairs_local, out_rank * in_rank).astype(jnp.bfloat16)
    query_rows = queries[0]
    gathered = lax.all_gather(sketch, "dp", axis=0, tiled=True)
    kernel, inner = lax.psum(
        (
            jnp.dot(gathered, gathered.T, preferred_element_type=jnp.float32),
            jnp.dot(gathered, query_rows.T, preferred_element_type=jnp.float32),
        ),
        "layer",
    )
    pair_total = kernel.shape[0]
    mean_diag = jnp.trace(kernel) / pair_total
    damping = damp_ratio * mean_diag
    factor = jnp.linalg.cholesky(kernel + damping * jnp.eye(pair_total, dtype=jnp.float32))
    solved = jax.scipy.linalg.cho_solve((factor, True), inner)
    own_rows = lax.dynamic_slice_in_dim(solved, lax.axis_index("dp") * pairs_local, pairs_local, 0)
    query_count = solved.shape[1]
    selected = query_index[:, :, None] == jnp.arange(query_count, dtype=jnp.int32)[None, None, :]
    picked = jnp.sum(jnp.where(selected, own_rows[:, None, :], jnp.float32(0.0)), axis=-1)
    scores = jnp.sqrt(mean_diag) * picked
    return (sketch[None], scores)


def solution(mesh):
    placed = (
        P("layer", "dp", None),
        P("layer", "dp", None),
        P("layer", "dp", None),
        P("layer", "dp", None),
        P("layer", None, None),
        P("dp", None),
        P("dp", None),
    )
    return jax.shard_map(
        local,
        mesh=mesh,
        in_specs=placed,
        out_specs=(P("layer", "dp", None), P("dp", None)),
        check_vma=False,
    )
```

profile of v0, /device:TPU:1, one launch (start us, length us, event | category | flops | bytes accessed | tf_op | source)
XLA Modules:
  0.0 687.6 jit_solution(17719228767692975417)
XLA Ops:
  7.2 1.6 copy.70
  8.9 0.7 copy.67
  9.6 255.2 %all_gather.9 = bf16[1,3584,64]{2,0,1:T(2,128)(2,1)} all-gather(bf16[1,28,64]{2,0,1:T(2,128)(2,1)S(1)} %copy.67), channel_id=1, replica_groups=mesh['dp'=128,'layer'=4] {'dp'}, dimensions={1}, use_global_device_ids=true | all-gather | bytes 462336 | tf_op jit(solution)/shard_map/all_gather | solution.py:26
  264.8 3.7 copy.68
  268.6 1.6 fusion.3
  270.4 10.6 %copy.71 = bf16[1,9728,64]{1,2,0:T(8,128)(2,1)} copy(bf16[1,9728,64]{2,0,1:T(2,128)(2,1)} %all-gather.4.cloned.1.call-done) | data formatting | bytes 2490368 | tf_op jit(solution)/shard_map/all_gather | solution.py:20
  281.0 2.2 fusion.4
  283.6 0.7 convert_element_type.38
  284.4 124.4 %all-gather.6.cloned.1.call-done = bf16[128,4,4096]{2,1,0:T(4,128)(2,1)} async-done(((bf16[1,4,4096]{2,1,0:T(4,128)(2,1)}), bf16[128,4,4096]{2,1,0:T(4,128)(2,1)}) %all-gather.6.cloned.1.call-update) | async-done | bytes 4194320 | tf_op jit(solution)/shard_map/all_gather | solution.py:43
  408.8 6.9 %reshape.118 = bf16[512,4096]{1,0:T(8,128)(2,1)} reshape(bf16[128,4,4096]{2,1,0:T(4,128)(2,1)} %all-gather.6.cloned.1.call-done) | data formatting | bytes 8388608
  415.7 6.9 %fusion.65 = f32[512,512]{0,1:T(8,128)} fusion(bf16[512,4096]{1,0:T(8,128)(2,1)} %reshape.118), kind=kOutput, calls=%fused_computation.112 | convolution fusion | flops 2147483648 | bytes 5242880 | tf_op jit(solution)/shard_map/dot_general | solution.py:46
  422.6 2.0 fusion.11
  425.2 68.9 %all-reduce.4.cloned.1.call-done = (f32[512,512]{0,1:T(8,128)}, f32[512,64]{0,1:T(8,128)}) async-done(((f32[512,512]{0,1:T(8,128)}, f32[512,64]{0,1:T(8,128)}), (f32[512,512]{0,1:T(8,128)}, f32[512,64]{0,1:T(8,128)})) %all-reduce.4.cloned.1.call-update) | async-done | bytes 1179664 | tf_op jit(solution)/shard_map/psum | solution.py:44
  494.1 2.0 select_reduce_fusion
  496.7 2.3 select_add_fusion
  499.0 2.6 copy.74
  501.6 1.4 fusion.9
  503.1 1.0 copy-done.3
  504.1 11.7 %cholesky.103 = f32[128,128]{1,0:T(8,128)S(1)} custom-call(f32[128,128]{1,0:T(8,128)S(1)} %cholesky.263), custom_call_target="Cholesky" | custom-call | tf_op jit(solution)/shard_map/jit(cholesky)/cholesky | solution.py:54
  515.8 9.8 %custom-call.34 = f32[1,128,128]{1,2,0:T(8,128)S(1)} custom-call(f32[1,128,128]{2,1,0:T(8,128)S(1)} %get-tuple-element.47), custom_call_target="InvertDiagBlocksLowerTriangular" | custom-call | tf_op jit(solution)/shard_map/jit(cholesky)/cholesky | solution.py:54
  525.6 1.2 fusion.18
  526.9 1.3 convolution_subtract_fusion
  528.2 0.7 copy-done.4
  528.8 11.9 %cholesky.215 = f32[128,128]{1,0:T(8,128)S(1)} custom-call(f32[128,128]{1,0:T(8,128)S(1)} %cholesky.267), custom_call_target="Cholesky" | custom-call | tf_op jit(solution)/shard_map/jit(cholesky)/cholesky | solution.py:54
  540.8 0.7 copy.77
  541.5 0.8 copy.76
  542.3 0.7 copy.75
  543.0 10.4 %custom-call.35 = f32[1,128,128]{1,2,0:T(8,128)} custom-call(f32[1,128,128]{2,1,0:T(8,128)S(1)} %get-tuple-element.45), custom_call_target="InvertDiagBlocksLowerTriangular" | custom-call | tf_op jit(solution)/shard_map/jit(cholesky)/cholesky | solution.py:54
  553.4 1.0 cholesky.222
  554.4 0.9 constant_dynamic-update-slice_fusion
  555.3 0.8 constant_dynamic-update-slice_fusion.3
  556.2 1.2 convolution_dynamic-update-slice_fusion
  557.4 1.5 convolution_subtract_fusion.1
  558.9 0.6 copy-done.6
  560.2 13.2 %cholesky.236 = f32[128,128]{1,0:T(8,128)} custom-call(f32[128,128]{1,0:T(8,128)} %cholesky.272), custom_call_target="Cholesky" | custom-call | tf_op jit(solution)/shard_map/jit(cholesky)/cholesky | solution.py:54
  573.4 1.5 select_reduce_fusion.2
  574.9 1.5 copy.79
  576.4 0.8 constant_dynamic-update-slice_fusion.1
  577.2 11.3 %custom-call.36 = f32[1,128,128]{1,2,0:T(8,128)} custom-call(f32[1,128,128]{2,1,0:T(8,128)} %get-tuple-element.43), custom_call_target="InvertDiagBlocksLowerTriangular" | custom-call | tf_op jit(solution)/shard_map/jit(cholesky)/cholesky | solution.py:54
  588.5 1.2 convolution_dynamic-update-slice_fusion.1
  589.7 1.9 convolution_subtract_fusion.2
  591.6 13.3 %cholesky.253 = f32[128,128]{1,0:T(8,128)} custom-call(f32[128,128]{1,0:T(8,128)} %convolution_subtract_fusion.2), custom_call_target="Cholesky" | custom-call | tf_op jit(solution)/shard_map/jit(cholesky)/cholesky | solution.py:54
  605.0 1.4 select_reduce_fusion.1
  606.4 1.6 copy.81
  608.5 1.2 compare_reduce_fusion
  609.7 0.8 constant_dynamic-update-slice_fusion.2
  610.6 0.7 compare_reduce_fusion.2
  613.6 1.1 select_select_fusion
  615.3 14.5 %while.1 = (s32[]{:T(128)}, f32[512,512]{0,1:T(8,128)}, s32[4,2]{0,1:T(2,128)S(1)}, f32[4,128,128]{2,1,0:T(8,128)}, s32[]{:T(128)}) while((s32[]{:T(128)}, f32[512,512]{0,1:T(8,128)}, s32[4,2]{0,1:T(2,128)S(1)}, f32[4,128,128]{2,1,0:T(8,128)}, s32[]{:T(128)}) %tuple.32), condition=%wide.while_cond, body=%wide.while_body.sunk | while | flops 2 | bytes 393829 | solution.py:55
  616.0 2.2 dynamic-slice.7
  618.4 0.6 bitcast_dynamic-update-slice_fusion.2
  619.7 2.2 dynamic-slice.7
  622.0 0.6 bitcast_dynamic-update-slice_fusion.2
  623.3 2.2 dynamic-slice.7
  625.7 0.6 bitcast_dynamic-update-slice_fusion.2
  627.0 2.2 dynamic-slice.7
  629.9 40.1 %custom-call.37 = f32[4,128,128]{1,2,0:T(8,128)S(1)} custom-call(f32[4,128,128]{2,1,0:T(8,128)} %get-tuple-element.9), custom_call_target="InvertDiagBlocksLowerTriangular" | custom-call | tf_op jit(solution)/shard_map/jit(_cho_solve)/triangular_solve | solution.py:55
  670.0 0.9 fusion.48
  671.0 1.0 convolution_subtract_fusion.8
  672.2 1.1 convolution_subtract_fusion.7
  673.5 1.2 convolution_subtract_fusion.6
  675.1 1.1 convolution_subtract_fusion.5
  676.5 1.2 convolution_subtract_fusion.4
  677.9 1.3 convolution_subtract_fusion.3
  (60 shorter events, 9.4 us)
Async XLA Ops:
  7.2 273.8 %copy-start = (bf16[1,128,9728]{2,1,0:T(8,128)(2,1)S(1)}, bf16[1,128,9728]{2,1,0:T(8,128)(2,1)}, u32[]{:S(2)}) copy-start(bf16[1,128,9728]{2,1,0:T(8,128)(2,1)} %param.7) | copy-start | bytes 7471108
  7.2 261.3 %copy-start.8 = (s32[1,4]{1,0:T(1,128)S(1)}, s32[1,4]{1,0:T(1,128)}, u32[]{:S(2)}) copy-start(s32[1,4]{1,0:T(1,128)} %param.12) | copy-start | bytes 52
  7.2 263.2 %all-gather.4.cloned.1.call-start = ((), (), s32[]{:S(2)}) async-start(), calls=%async_computation | async-start | bytes 5019648 | tf_op jit(solution)/shard_map/all_gather | solution.py:20
  8.8 399.9 %all-gather.6.cloned.1.call-start = ((), (), s32[]{:S(2)}) async-start(), calls=%async_computation.1 | async-start | bytes 4227072 | tf_op jit(solution)/shard_map/all_gather | solution.py:43
  284.3 209.8 %all-reduce.4.cloned.1.call-start = ((), (), s32[]{:S(2)}) async-start(), calls=%async_computation.2 | async-start | bytes 2359296 | tf_op jit(solution)/shard_map/psum | solution.py:44
  415.7 6.9 %copy-start.1 = (bf16[512,4096]{1,0:T(8,128)(2,1)S(1)}, bf16[512,4096]{1,0:T(8,128)(2,1)}, u32[]{:S(2)}) copy-start(bf16[512,4096]{1,0:T(8,128)(2,1)} %reshape.118) | copy-start | bytes 12582916
  415.7 6.9 %copy-start.5 = (bf16[1,64,4096]{2,1,0:T(8,128)(2,1)S(1)}, bf16[1,64,4096]{2,1,0:T(8,128)(2,1)}, u32[]{:S(2)}) copy-start(bf16[1,64,4096]{2,1,0:T(8,128)(2,1)} %param.11) | copy-start | bytes 1572868
  494.1 7.5 %copy-start.2 = (f32[512,512]{0,1:T(8,128)S(1)}, f32[512,512]{0,1:T(8,128)}, u32[]{:S(2)}) copy-start(f32[512,512]{0,1:T(8,128)} %get-tuple-element.38) | copy-start | bytes 3145732
  503.1 1.0 copy-start.3
  528.1 0.7 copy-start.4
  558.9 0.6 copy-start.6
  560.2 120.1 %copy-start.7 = (s32[4,8]{1,0:T(4,128)S(1)}, s32[4,8]{1,0:T(4,128)}, u32[]{:S(2)}) copy-start(s32[4,8]{1,0:T(4,128)} %param.13) | copy-start | bytes 388
Sparse Core Ops, SparseCore 0:
  12.7 147.1 all-gather.3
  284.5 124.2 all-gather.5
  424.8 69.2 all-reduce.3
where the time goes:
time: 690 us; the launch traced here: 688 us
  blocking collectives  255 us (37%)
  waiting for transfers between devices  193 us (28%)
  other arithmetic  135 us (20%)
  local copies, waits for them, and re-layouts  55 us (8%)
  matrix products  30.7 us (4%)
  between operations  17.6 us (3%)
    all_gather x1, blocking collectives, local(): lax.all_gather(out_basis, 'dp', axis=1, tiled=True)[0]  255 us
    all_gather x1, waiting for transfers between devices, local(): gathered = lax.all_gather(sketch, 'dp', axis=0, tiled=True)  124 us
    another operation x14, other arithmetic, local(): jnp.linalg.cholesky(kernel + damping * jnp.eye(pair_total, dtype=jnp.floa...  87.1 us
    psum x1, waiting for transfers between devices, local(): lax.psum((jnp.dot(gathered, gathered.T, preferred_element_type=jnp.float3...  68.9 us
    another operation x4, other arithmetic, local(): solved = jax.scipy.linalg.cho_solve((factor, True), inner)  41.9 us
    another operation x20, local copies, waits for them, and re-layouts  14.5 us
  transfers between devices with their start and end apart: 3, of which 2 were waited for; matrix products, arithmetic and copies ran while one was open for 1% of the time, Pallas kernels for 0%

commit v1 on v0

v1 whole, which is shorter than its diff:
```python
import jax
import jax.numpy as jnp
from jax import lax
from jax.experimental import pallas as pl
from jax.experimental.pallas import tpu as pltpu
from jax.sharding import PartitionSpec as P

MESH = pl.DeviceIdType.MESH
damp_ratio = 0.5
F32 = jnp.float32
BF16 = jnp.bfloat16
NT = (((1,), (1,)), ((), ()))
SEMS = 128


def iota(shape, dim):
    return lax.broadcasted_iota(jnp.int32, shape, dim)


def onehot(cond):
    return jnp.where(cond, 1.0, 0.0).astype(BF16)


def pieces(v):
    hi = v.astype(BF16)
    rest = v - hi.astype(F32)
    mid = rest.astype(BF16)
    return hi, mid, (rest - mid.astype(F32)).astype(BF16)


def dot(a, b):
    return jnp.dot(a, b, preferred_element_type=F32)


def dot_nt(a, b):
    return lax.dot_general(a, b, NT, preferred_element_type=F32)


def front(act, grd, wblk, qblk, lens, sk, kin, av, gv, xs, wg, srow, scol, lx, kb, perm, acc, in_sem, ssem, rsem):
    me = lax.axis_index("dp")
    ly = lax.axis_index("layer")
    c = me % 2
    h = (me // 2) % 2
    x = (me // 4) % 4
    z = me // 16
    b = me % 16

    def at(zz, xx, hh, cc):
        return ((zz * 4 + xx) * 2 + hh) * 2 + cc

    h_peer = at(z, x, 1 - h, c)
    c_peer = at(z, x, h, 1 - c)
    x_peers = [at(z, (x + d) % 4, h, c) for d in range(1, 4)]
    z_peers = [at((z + d) % 8, x, h, c) for d in range(1, 8)]

    load_a = pltpu.make_async_copy(act, av, in_sem.at[0])
    load_g = pltpu.make_async_copy(grd, gv, in_sem.at[1])
    load_a.start()
    load_g.start()

    barrier = pltpu.get_barrier_semaphore()
    for peer in [h_peer, c_peer] + x_peers + z_peers:
        pl.semaphore_signal(barrier, inc=1, device_id={"dp": peer}, device_id_type=MESH)
    for d in range(1, 4):
        pl.semaphore_signal(barrier, inc=1, device_id={"layer": (ly + d) % 4}, device_id_type=MESH)

    used = [0]
    sent = []

    def take():
        used[0] += 1
        return used[0] - 1

    def send(src, dst, sem, device):
        copy = pltpu.make_async_remote_copy(
            src_ref=src, dst_ref=dst, send_sem=ssem.at[sem], recv_sem=rsem.at[sem], device_id=device, device_id_type=MESH
        )
        copy.start()
        sent.append(copy)

    def arrived(slot, sem):
        pltpu.make_async_remote_copy(
            src_ref=slot, dst_ref=slot, send_sem=ssem.at[sem], recv_sem=rsem.at[sem], device_id={"dp": c_peer}, device_id_type=MESH
        ).wait_recv()

    def ring(slot, forward_own, step_work):
        right = {"dp": at((z + 1) % 8, x, h, c)}
        left = {"dp": at((z + 7) % 8, x, h, c)}
        other = {"dp": c_peer}
        names = {}

        def name(kind, s, q):
            if (kind, s, q) not in names:
                names[(kind, s, q)] = take()
            return names[(kind, s, q)]

        def goes(kind, s, q):
            return s < 4 or (kind == "r" and q == 0) or (kind == "l" and q == 1)

        def place(kind, s):
            return (z + 8 - s) % 8 if kind == "r" else (z + s) % 8

        def pass_on(kind, s, q):
            target = right if kind == "r" else left
            ref = slot(c, place(kind, s - 1), q)
            send(ref, ref, name(kind, s, q), target)

        def hand(kind, s, q):
            ref = slot(c, place(kind, s), q)
            send(ref, ref, name("f" + kind, s, q), other)

        for q in range(2):
            pass_on("r", 1, q)
            pass_on("l", 1, q)
        if forward_own:
            for q in range(2):
                hand("r", 0, q)
        step_work(0, [(z, 0), (z, 1)], [])
        pending = [("r", 0, 0), ("r", 0, 1)] if forward_own else []
        for s in range(1, 5):
            got = []
            for q in range(2):
                for kind in ("r", "l"):
                    if not goes(kind, s, q):
                        continue
                    arrived(slot(c, place(kind, s), q), name(kind, s, q))
                    if s < 4 and goes(kind, s + 1, q):
                        pass_on(kind, s + 1, q)
                    hand(kind, s, q)
                    got.append((kind, s, q))
            for kind, t, q in pending:
                arrived(slot(1 - c, place(kind, t), q), name("f" + kind, t, q))
            step_work(s, [(place(k, t), q) for k, t, q in got], [(place(k, t), q) for k, t, q in pending])
            pending = got
        for kind, t, q in pending:
            arrived(slot(1 - c, place(kind, t), q), name("f" + kind, t, q))
        step_work(5, [], [(place(k, t), q) for k, t, q in pending])

    scol[8] = qblk[...]
    lane = iota((128, 512), 0)
    col = iota((128, 512), 1)
    for j in range(16):
        perm[pl.ds(128 * j, 128), :] = onehot(col == ((lane // 4) % 8) * 64 + j * 4 + lane % 4)
    acc[...] = jnp.zeros_like(acc)

    pl.semaphore_wait(barrier, 15)
    own = wg.at[c, z, x, h]
    w_h = take()
    send(wblk, own, w_h, {"dp": h_peer})
    wg[c, z, x, h] = wblk[...]
    load_a.wait()
    load_g.wait()

    sel_r = iota((256, 128), 0)
    sel_c = iota((256, 128), 1)

    def prepare(lo, hi):
        def body(part, carry):
            zl = part // 4
            xx = part % 4
            for hh in range(2):
                for cc in range(2):
                    i0 = zl * 16 + xx * 4 + hh * 2 + cc
                    ta = jnp.minimum((76 * i0) // 128, 17)
                    oa = 76 * i0 - 128 * ta
                    tg = jnp.minimum((28 * i0) // 128, 5)
                    og = 28 * i0 - 128 * tg
                    sel_a = onehot((sel_r == sel_c + oa) & (sel_c < 76))
                    sel_g = onehot((sel_r == sel_c - 76 + og) & (sel_c >= 76) & (sel_c < 104))
                    a4 = jnp.concatenate(
                        [av[:, pl.ds(pl.multiple_of((ta + 19 * n) * 128, 128), 256)] for n in range(4)], axis=0
                    )
                    g4 = jnp.concatenate(
                        [gv[:, pl.ds(pl.multiple_of((tg + 7 * n) * 128, 128), 256)] for n in range(4)], axis=0
                    )
                    xa = dot(a4, sel_a).astype(BF16)
                    xg = dot(g4, sel_g).astype(BF16)
                    q = xx // 2
                    off = pl.multiple_of(((xx % 2) * 2 + hh) * 128, 128)
                    for n in range(4):
                        xs[cc, 2 * n + zl, q, 0:128, pl.ds(off, 128)] = xa[128 * n : 128 * n + 128]
                        xs[cc, 2 * n + zl, q, 128:256, pl.ds(off, 128)] = xg[128 * n : 128 * n + 128]
            return carry

        lax.fori_loop(lo, hi, body, 0)

    prepare(0, 2)
    arrived(wg.at[c, z, x, 1 - h], w_h)
    w_x = [take() for _ in range(3)]
    for d in range(3):
        send(wg.at[c, z, x], wg.at[c, z, x], w_x[d], {"dp": x_peers[d]})
    prepare(2, 4)
    for d in range(3):
        arrived(wg.at[c, z, (x + 3 - d) % 4], w_x[d])

    def multiply(color, zz, q):
        w = wg[color, zz, pl.ds(2 * q, 2)]
        wide = jnp.concatenate([w[0, 0], w[0, 1], w[1, 0], w[1, 1]], axis=1)
        acc[...] += dot_nt(xs[color, zz, q], wide)

    def project(s, mine, theirs):
        if s == 0:
            prepare(4, 8)
        for zz, q in mine:
            multiply(c, zz, q)
        for zz, q in theirs:
            multiply(1 - c, zz, q)

    ring(lambda cc, zz, q: wg.at[cc, zz, pl.ds(2 * q, 2)], True, project)

    tok = iota((128, 64), 0)
    length = jnp.zeros((128, 64), jnp.int32)
    for p in range(4):
        length = jnp.where(tok // 32 == p, lens[0, p], length)
    mask = jnp.where(tok % 32 < length, 1.0, 0.0).astype(F32)
    right_proj = acc[0:128].astype(BF16)
    left_proj = (mask * acc[128:256]).astype(BF16)
    row = iota((128, 128), 0)
    colm = iota((128, 128), 1)
    mine = jnp.where(colm // 32 == row % 4, 1.0, 0.0).astype(F32)
    k_row = iota((128, 64), 0)
    k_col = iota((128, 64), 1)
    j_row = iota((64, 128), 0)
    j_col = iota((64, 128), 1)
    total = jnp.zeros((128, 128), F32)
    for par in range(2):
        spread = dot_nt(onehot(k_col == 2 * (k_row // 4) + par), left_proj)
        lefts = (spread * mine).astype(BF16)
        rights = dot(right_proj, onehot(j_col == j_row + 64 * par)).astype(BF16)
        total = total + dot(lefts, rights)
    sketch = total.astype(BF16)
    sk[...] = sketch
    srow[c, x, h] = sketch
    scol[z] = sketch

    s_h = take()
    send(srow.at[c, x, h], srow.at[c, x, h], s_h, {"dp": h_peer})
    s_z = [take() for _ in range(7)]
    for d in range(7):
        send(scol.at[z], scol.at[z], s_z[d], {"dp": z_peers[d]})
    arrived(srow.at[c, x, 1 - h], s_h)
    s_x = [take() for _ in range(3)]
    s_c = [take() for _ in range(4)]
    for d in range(3):
        send(srow.at[c, x], srow.at[c, x], s_x[d], {"dp": x_peers[d]})
    send(srow.at[c, x], srow.at[c, x], s_c[0], {"dp": c_peer})
    for d in range(3):
        xx = (x + 3 - d) % 4
        arrived(srow.at[c, xx], s_x[d])
        send(srow.at[c, xx], srow.at[c, xx], s_c[d + 1], {"dp": c_peer})
    for d in range(7):
        arrived(scol.at[(z + 7 - d) % 8], s_z[d])
    for d in range(4):
        arrived(srow.at[1 - c, (x + 4 - d) % 4], s_c[d])

    gram = jnp.zeros((256, 144), F32)
    for u in range(4):
        rows = [srow[:, :, :, pl.ds(32 * u + 16 * v, 16), :].reshape(256, 128) for v in range(2)]
        cols = [scol[:, pl.ds(32 * u + 16 * v, 16), :].reshape(144, 128) for v in range(2)]
        gram = gram + dot_nt(jnp.concatenate(rows, axis=1), jnp.concatenate(cols, axis=1))
    gr = iota((256, 144), 0)
    gc = iota((256, 144), 1)
    gram = jnp.where((gr // 4) % 4 == (gc // 4) % 4, gram, 0.0)
    pr = iota((64, 256), 0)
    pc = iota((64, 256), 1)
    blk = pc // 16
    pick_rows = onehot(pr == ((blk // 2) % 4) * 16 + (blk % 2) * 8 + (blk // 8) * 4 + pc % 4)
    half = sum(dot(pick_rows, v) for v in pieces(gram))
    nr = iota((144, 256), 0)
    nc = iota((144, 256), 1)
    in_k = (nr < 128) & (nc < 128) & (nc % 32 == (nr // 16) * 4 + nr % 4)
    in_q = (nr >= 128) & (nc >= 128) & ((nc - 128) // 16 == b % 8) & (nc % 4 == nr % 4)
    pick_cols = onehot(in_k | in_q)
    spread = sum(dot(v, pick_cols) for v in pieces(half))
    yr = iota((64, 256), 0)
    yc = iota((64, 256), 1)
    quarter = jnp.where(yc < 128, yc // 32, (yc // 4) % 4) == yr // 16
    spread = jnp.where(quarter, spread, 0.0)
    lx[ly] = spread[0:16] + spread[16:32] + spread[32:48] + spread[48:64]

    l_s = [take() for _ in range(3)]
    for d in range(3):
        send(lx.at[ly], lx.at[ly], l_s[d], {"layer": (ly + 1 + d) % 4})
    for d in range(3):
        arrived(lx.at[(ly + 3 - d) % 4], l_s[d])
    kb[c, x, h] = (lx[0] + lx[1]) + (lx[2] + lx[3])

    k_h = take()
    send(kb.at[c, x, h], kb.at[c, x, h], k_h, {"dp": h_peer})
    arrived(kb.at[c, x, 1 - h], k_h)
    k_x = [take() for _ in range(3)]
    k_c = [take() for _ in range(4)]
    for d in range(3):
        send(kb.at[c, x], kb.at[c, x], k_x[d], {"dp": x_peers[d]})
    send(kb.at[c, x], kb.at[c, x], k_c[0], {"dp": c_peer})
    for d in range(3):
        xx = (x + 3 - d) % 4
        arrived(kb.at[c, xx], k_x[d])
        send(kb.at[c, xx], kb.at[c, xx], k_c[d + 1], {"dp": c_peer})
    for d in range(4):
        arrived(kb.at[1 - c, (x + 4 - d) % 4], k_c[d])

    def tall(v):
        return jnp.concatenate([v, v, v, v], axis=0)

    r4 = iota((64, 128), 0) // 16
    l4 = iota((64, 128), 1)
    wide = []
    side = [jnp.zeros((16, 128), F32), jnp.zeros((16, 128), F32)]
    for j in range(16):
        v = kb[j % 2, j // 4, (j // 2) % 2]
        wide.append(jnp.where(l4 // 32 == r4, tall(v[:, 0:128]), 0.0))
        side[j // 8] = side[j // 8] + v[:, 128:256]
    flat = jnp.concatenate(wide, axis=1)
    part = sum(dot(v, perm[...]) for v in pieces(flat))
    sides = jnp.concatenate([jnp.where((l4 // 4) % 4 == r4, tall(v), 0.0) for v in side], axis=1)
    ir = iota((256, 128), 0)
    ic = iota((256, 128), 1)
    place_q = onehot(ic == (ir // 16) * 4 + ir % 4)
    part_q = sum(dot(v, place_q) for v in pieces(sides))
    for cc in range(2):
        kin[z, cc, :, 0:512] = part[32 * cc : 32 * cc + 32]
        kin[z, cc, :, 512:640] = part_q[32 * cc : 32 * cc + 32]
    ring(lambda cc, zz, q: kin.at[zz, cc, pl.ds(16 * q, 16)], False, lambda s, mine, theirs: None)
    for copy in sent:
        copy.wait_send()


def run_front(act, grd, wblk, qblk, lens):
    vmem = pl.BlockSpec(memory_space=pltpu.VMEM)
    hbm = pl.BlockSpec(memory_space=pl.ANY)
    return pl.pallas_call(
        front,
        out_shape=(jax.ShapeDtypeStruct((128, 128), BF16), jax.ShapeDtypeStruct((8, 2, 32, 640), F32)),
        in_specs=[hbm, hbm, vmem, vmem, pl.BlockSpec(memory_space=pltpu.SMEM)],
        out_specs=(vmem, vmem),
        scratch_shapes=[
            pltpu.VMEM(act.shape, BF16),
            pltpu.VMEM(grd.shape, BF16),
            pltpu.VMEM((2, 8, 2, 256, 512), BF16),
            pltpu.VMEM((2, 8, 4, 2, 64, 128), BF16),
            pltpu.VMEM((2, 4, 2, 128, 128), BF16),
            pltpu.VMEM((9, 128, 128), BF16),
            pltpu.VMEM((4, 16, 256), F32),
            pltpu.VMEM((2, 4, 2, 16, 256), F32),
            pltpu.VMEM((2048, 512), BF16),
            pltpu.VMEM((256, 64), F32),
            pltpu.SemaphoreType.DMA((2,)),
            pltpu.SemaphoreType.DMA((SEMS,)),
            pltpu.SemaphoreType.DMA((SEMS,)),
        ],
        compiler_params=pltpu.CompilerParams(collective_id=0, has_side_effects=True, vmem_limit_bytes=48 * 1024 * 1024),
        name="front",
    )(act, grd, wblk, qblk, lens)


def solve(whole, query_index):
    kernel = whole[:, :512]
    inner = whole[:, 512:576]
    pair_total = kernel.shape[0]
    mean_diag = jnp.trace(kernel) / pair_total
    damping = damp_ratio * mean_diag
    factor = jnp.linalg.cholesky(kernel + damping * jnp.eye(pair_total, dtype=F32))
    solved = jax.scipy.linalg.cho_solve((factor, True), inner)
    own_rows = lax.dynamic_slice_in_dim(solved, lax.axis_index("dp") * 4, 4, 0)
    selected = query_index[:, :, None] == jnp.arange(64, dtype=jnp.int32)[None, None, :]
    picked = jnp.sum(jnp.where(selected, own_rows[:, None, :], jnp.float32(0.0)), axis=-1)
    return jnp.sqrt(mean_diag) * picked


def local(activations, out_grads, in_basis, out_basis, queries, pair_lengths, query_index):
    wblk = jnp.concatenate([in_basis[0].T, out_basis[0].T, jnp.zeros((64, 24), BF16)], axis=1)
    first = (lax.axis_index("dp") % 16) * 4
    qrows = lax.dynamic_slice_in_dim(queries[0], first, 4, 0)
    qblk = qrows.reshape(4, 32, 128).transpose(1, 0, 2).reshape(128, 128)
    sk, kin = run_front(activations[0], out_grads[0], wblk, qblk, pair_lengths)
    sketch = sk.reshape(32, 4, 128).transpose(1, 0, 2).reshape(1, 4, 4096)
    return sketch, solve(kin.reshape(512, 640), query_index)


def solution(mesh):
    placed = (
        P("layer", "dp", None),
        P("layer", "dp", None),
        P("layer", "dp", None),
        P("layer", "dp", None),
        P("layer", None, None),
        P("dp", None),
        P("dp", None),
    )
    return jax.shard_map(
        local,
        mesh=mesh,
        in_specs=placed,
        out_specs=(P("layer", "dp", None), P("dp", None)),
        check_vma=False,
    )
```

time: 690 us -> 255 us (0.37)
  blocking collectives: 255 us -> 0 us
  waiting for transfers between devices: 193 us -> 0 us
  Pallas kernels: 0 us -> 86.3 us
  local copies, waits for them, and re-layouts: 55 us -> 24.4 us
  matrix products: 30.7 us -> 11.2 us
  between operations: 17.6 us -> 5.25 us
  other arithmetic: 135 us -> 124 us
    all_gather x1 -> x0, blocking collectives: 255 us -> none  [local(): lax.all_gather(out_basis, 'dp', axis=1, tiled=True)[0]]
    all_gather x2 -> x0, waiting for transfers between devices: 124 us -> none  [the longest x1 124 us: local(): gathered = lax.all_gather(sketch, 'dp', axis=0, tiled=True)]
    pallas_call x0 -> x1, Pallas kernels: none -> 86.3 us  [run_front(): pl.pallas_call(front, out_shape=(jax.ShapeDtypeStruct((128, 128), BF16),...]
    psum x1 -> x0, waiting for transfers between devices: 68.9 us -> none  [local(): lax.psum((jnp.dot(gathered, gathered.T, preferred_element_type=jnp.float3...]
    all_gather x2 -> x0, local copies, waits for them, and re-layouts: 14.3 us -> none  [the longest x1 10.6 us: local(): lax.all_gather(in_basis, 'dp', axis=1, tiled=True)[0]]
    dot_general x5 -> x0, matrix products: 13 us -> none  [the longest x1 6.93 us: local(): jnp.dot(gathered, gathered.T, preferred_element_type=jnp.float32)]
    another operation x34 -> x35, local copies, waits for them, and re-layouts: 25.5 us -> 12.7 us
    another operation x18, other arithmetic: 129 us -> 119 us  [the longest x14 78.7 us: solve(): jnp.linalg.cholesky(kernel + damping * jnp.eye(pair_total, dtype=F32))]
  transfers between devices with their start and end apart: 3 -> 0, of which waited for: 2 -> 0; matrix products, arithmetic and copies ran while one was open for 1% -> 0% of each run, Pallas kernels for 0% -> 0%
where the time goes in v1:
time: 255 us; the launch traced here: 251 us
  other arithmetic  124 us (49%)
  Pallas kernels  86.3 us (34%)
  local copies, waits for them, and re-layouts  24.4 us (10%)
  matrix products  11.2 us (4%)
  between operations  5.25 us (2%)
    pallas_call x1, Pallas kernels, run_front(): pl.pallas_call(front, out_shape=(jax.ShapeDtypeStruct((128, 128), BF16),...  86.3 us
    another operation x14, other arithmetic, solve(): jnp.linalg.cholesky(kernel + damping * jnp.eye(pair_total, dtype=F32))  78.7 us
    another operation x4, other arithmetic, solve(): solved = jax.scipy.linalg.cho_solve((factor, True), inner)  40.6 us
    another operation x20, local copies, waits for them, and re-layouts  12 us
    unnamed x20, local copies, waits for them, and re-layouts  7.79 us
    another operation x6, matrix products, solve(): jnp.linalg.cholesky(kernel + damping * jnp.eye(pair_total, dtype=F32))  6.09 us
    another operation x14, matrix products, solve(): solved = jax.scipy.linalg.cho_solve((factor, True), inner)  5.12 us

profile of v1, /device:TPU:1, one launch (start us, length us, event | category | flops | bytes accessed | tf_op | source)
XLA Modules:
  0.0 251.4 jit_solution(2702562984319186977)
XLA Ops:
  0.6 0.9 copy.35
  1.6 0.8 maximum_maximum_fusion.wblk
  2.4 1.7 copy-done.1
  4.1 1.2 copy-done.2
  5.3 0.7 copy-done.3
  6.0 86.3 %front.1 = (bf16[128,128]{1,0:T(8,128)(2,1)S(1)}, f32[8,2,32,640]{3,2,1,0:T(8,128)S(1)}) custom-call(bf16[128,9728]{1,0:T(8,128)(2,1)S(1)} %bitcast.74, bf16[128,3584]{1,0:T(8,128)(2,1)S(1)} %bitcast.78, bf16[64,128]{1,0:T(8,128)(2,1)S(1)} %maximum_maximum_fusion.wblk, bf16[128,128]{1,0:T(8,128)(2,1)S(1)} %bitcast.79, s32[1,4]{1,0:T(1,128)S(1)} %copy-done.3), custom_call_target="tpu_custom_call" | custom-call | tf_op jit(solution)/shard_map/front/pallas_call | solution.py:332
  92.3 1.1 slice.167
  93.4 1.6 copy.54
  95.0 0.7 select_reduce_fusion
  96.3 1.1 select_add_fusion
  97.4 2.6 %copy.38 = f32[512,512]{1,0:T(8,128)} copy(f32[512,512]{0,1:T(8,128)} %select_add_fusion) | data formatting | bytes 2097152 | tf_op jit(solution)/shard_map/add | solution.py:363
  100.0 1.4 fusion
  101.5 1.0 copy-done.5
  102.5 11.7 %cholesky.103 = f32[128,128]{1,0:T(8,128)S(1)} custom-call(f32[128,128]{1,0:T(8,128)S(1)} %cholesky.263), custom_call_target="Cholesky" | custom-call | tf_op jit(solution)/shard_map/jit(cholesky)/cholesky | solution.py:363
  114.2 0.1 copy.39
  114.3 0.1 cholesky.222
  114.5 9.8 %custom-call.34 = f32[1,128,128]{1,2,0:T(8,128)S(1)} custom-call(f32[1,128,128]{2,1,0:T(8,128)S(1)} %get-tuple-element.44), custom_call_target="InvertDiagBlocksLowerTriangular" | custom-call | tf_op jit(solution)/shard_map/jit(cholesky)/cholesky | solution.py:363
  124.3 1.4 fusion.5
  125.7 0.1 copy.40
  125.9 1.3 convolution_subtract_fusion
  127.1 11.7 %cholesky.215 = f32[128,128]{1,0:T(8,128)S(1)} custom-call(f32[128,128]{1,0:T(8,128)S(1)} %cholesky.267), custom_call_target="Cholesky" | custom-call | tf_op jit(solution)/shard_map/jit(cholesky)/cholesky | solution.py:363
  138.9 0.1 copy.41
  139.0 9.8 %custom-call.35 = f32[1,128,128]{1,2,0:T(8,128)S(1)} custom-call(f32[1,128,128]{2,1,0:T(8,128)S(1)} %get-tuple-element.42), custom_call_target="InvertDiagBlocksLowerTriangular" | custom-call | tf_op jit(solution)/shard_map/jit(cholesky)/cholesky | solution.py:363
  148.8 0.3 convolution_dynamic-update-slice_fusion
  149.1 1.5 convolution_subtract_fusion.1
  150.7 11.7 %cholesky.236 = f32[128,128]{1,0:T(8,128)S(1)} custom-call(f32[128,128]{1,0:T(8,128)S(1)} %cholesky.272), custom_call_target="Cholesky" | custom-call | tf_op jit(solution)/shard_map/jit(cholesky)/cholesky | solution.py:363
  162.4 0.1 copy.43
  162.5 10.0 %custom-call.36 = f32[1,128,128]{1,2,0:T(8,128)S(1)} custom-call(f32[1,128,128]{2,1,0:T(8,128)S(1)} %get-tuple-element.40), custom_call_target="InvertDiagBlocksLowerTriangular" | custom-call | tf_op jit(solution)/shard_map/jit(cholesky)/cholesky | solution.py:363
  172.5 0.3 convolution_dynamic-update-slice_fusion.1
  172.8 1.3 convolution_subtract_fusion.2
  174.2 11.7 %cholesky.253 = f32[128,128]{1,0:T(8,128)S(1)} custom-call(f32[128,128]{1,0:T(8,128)S(1)} %convolution_subtract_fusion.2), custom_call_target="Cholesky" | custom-call | tf_op jit(solution)/shard_map/jit(cholesky)/cholesky | solution.py:363
  185.9 0.1 copy.45
  186.0 0.7 compare_reduce_fusion.2
  187.9 0.7 compare_reduce_fusion.1
  189.4 0.7 compare_reduce_fusion
  190.8 1.1 select_select_fusion
  191.9 12.1 %while.1 = (s32[]{:T(128)}, f32[512,512]{0,1:T(8,128)}, s32[4,2]{0,1:T(2,128)S(1)}, f32[4,128,128]{2,1,0:T(8,128)S(1)}, s32[]{:T(128)}) while((s32[]{:T(128)}, f32[512,512]{0,1:T(8,128)}, s32[4,2]{0,1:T(2,128)S(1)}, f32[4,128,128]{2,1,0:T(8,128)S(1)}, s32[]{:T(128)}) %tuple.32), condition=%wide.while_cond, body=%wide.while_body.sunk | while | flops 2 | bytes 393329 | solution.py:364
  192.0 0.6 fusion.63
  192.6 2.2 dynamic-slice.8
  195.1 0.6 fusion.63
  195.7 2.2 dynamic-slice.8
  198.1 0.6 fusion.63
  198.7 2.2 dynamic-slice.8
  201.2 0.6 fusion.63
  201.8 2.2 dynamic-slice.8
  204.1 39.3 %custom-call.37 = f32[4,128,128]{1,2,0:T(8,128)S(1)} custom-call(f32[4,128,128]{2,1,0:T(8,128)S(1)} %get-tuple-element.13), custom_call_target="InvertDiagBlocksLowerTriangular" | custom-call | tf_op jit(solution)/shard_map/jit(_cho_solve)/triangular_solve | solution.py:364
  243.4 0.3 fusion.23
  244.0 1.0 convolution_subtract_fusion.8
  245.0 0.2 fusion.38
  245.2 1.1 convolution_subtract_fusion.7
  246.3 0.2 fusion.40
  246.5 0.3 convolution_subtract_fusion.6
  246.8 0.2 fusion.42
  247.0 0.2 fusion.41
  247.3 0.2 convolution_subtract_fusion.5
  247.5 0.2 fusion.39
  247.8 0.3 convolution_subtract_fusion.4
  248.0 0.2 fusion.37
  248.3 0.4 convolution_subtract_fusion.3
  248.7 0.2 fusion.36
  248.9 0.1 fusion.45
  249.1 0.2 select_reduce_fusion.5
  250.0 0.6 broadcast_multiply_fusion
  250.6 0.6 copy.75
  (44 shorter events, 1.4 us)
Async XLA Ops:
  0.6 1.8 copy-start
  2.4 1.7 copy-start.1
  4.1 1.2 copy-start.2
  5.3 0.7 copy-start.3
  101.5 1.0 copy-start.5
  204.1 42.4 %copy-start.4 = (f32[512,512]{0,1:T(8,128)S(1)}, f32[512,512]{0,1:T(8,128)}, u32[]{:S(2)}) copy-start(f32[512,512]{0,1:T(8,128)} %get-tuple-element.95) | copy-start | bytes 3145732
  244.0 5.2 %copy-start.6 = (s32[4,8]{1,0:T(4,128)S(1)}, s32[4,8]{1,0:T(4,128)}, u32[]{:S(2)}) copy-start(s32[4,8]{1,0:T(4,128)} %param.13) | copy-start | bytes 388

commit v2 on v1

--- a/solution.py
+++ b/solution.py
@@ -10,7 +10,7 @@
 F32 = jnp.float32
 BF16 = jnp.bfloat16
 NT = (((1,), (1,)), ((), ()))
-SEMS = 128
+SEMS = 160
 
 
 def iota(shape, dim):
@@ -36,7 +36,7 @@
     return lax.dot_general(a, b, NT, preferred_element_type=F32)
 
 
-def front(act, grd, wblk, qblk, lens, sk, kin, av, gv, xs, wg, srow, scol, lx, kb, perm, acc, in_sem, ssem, rsem):
+def front(act, grd, inb_hbm, outb_hbm, qry_hbm, lens_hbm, sk, kin, av, gv, inb, outb, qry, lens, xs, wa, wb, srow, scol, lx, kb, perm, acc, in_sem, ssem, rsem):
     me = lax.axis_index("dp")
     ly = lax.axis_index("layer")
     c = me % 2
@@ -55,14 +55,20 @@
 
     load_a = pltpu.make_async_copy(act, av, in_sem.at[0])
     load_g = pltpu.make_async_copy(grd, gv, in_sem.at[1])
-    load_a.start()
-    load_g.start()
+    load_l = pltpu.make_async_copy(lens_hbm, lens, in_sem.at[2])
+    load_i = pltpu.make_async_copy(inb_hbm, inb, in_sem.at[3])
+    load_o = pltpu.make_async_copy(outb_hbm, outb, in_sem.at[4])
+    load_q = pltpu.make_async_copy(qry_hbm, qry, in_sem.at[5])
+    for load in (load_i, load_o, load_a, load_g, load_q, load_l):
+        load.start()
 
     barrier = pltpu.get_barrier_semaphore()
     for peer in [h_peer, c_peer] + x_peers + z_peers:
         pl.semaphore_signal(barrier, inc=1, device_id={"dp": peer}, device_id_type=MESH)
     for d in range(1, 4):
-        pl.semaphore_signal(barrier, inc=1, device_id={"layer": (ly + d) % 4}, device_id_type=MESH)
+        for hh in range(2):
+            peer = {"dp": at(z, x, (h + hh) % 2, c), "layer": (ly + d) % 4}
+            pl.semaphore_signal(barrier, inc=1, device_id=peer, device_id_type=MESH)
 
     used = [0]
     sent = []
@@ -136,20 +142,41 @@
             arrived(slot(1 - c, place(kind, t), q), name("f" + kind, t, q))
         step_work(5, [], [(place(k, t), q) for k, t, q in pending])
 
-    scol[8] = qblk[...]
-    lane = iota((128, 512), 0)
-    col = iota((128, 512), 1)
-    for j in range(16):
-        perm[pl.ds(128 * j, 128), :] = onehot(col == ((lane // 4) % 8) * 64 + j * 4 + lane % 4)
+    eye = onehot(iota((64, 64), 0) == iota((64, 64), 1))
+    load_i.wait()
+    load_o.wait()
+    out_t = dot_nt(eye, outb[...]).astype(BF16)
+    in_at = onehot(iota((76, 128), 0) == iota((76, 128), 1))
+    out_at = onehot(iota((28, 128), 0) + 76 == iota((28, 128), 1))
+    own = (dot(inb[...], in_at) + dot(out_t, out_at)).astype(BF16)
+
+    @pl.when(c == 0)
+    def _():
+        wa[z, x, h] = own
+
+    @pl.when(c == 1)
+    def _():
+        wb[x, h, z] = own
+
+    def tables():
+        load_q.wait()
+        q_row = iota((8, 64), 0)
+        q_col = iota((8, 64), 1)
+        low = onehot((q_row < 4) & (q_col == 4 * b + q_row))
+        high = onehot((q_row >= 4) & (q_col == 4 * b + q_row - 4))
+        tiles = [
+            dot(low, qry[:, 256 * i : 256 * i + 128]) + dot(high, qry[:, 256 * i + 128 : 256 * i + 256]) for i in range(16)
+        ]
+        scol[8] = jnp.concatenate(tiles, axis=0).astype(BF16)
+        lane = iota((128, 512), 0)
+        col = iota((128, 512), 1)
+        for j in range(16):
+            perm[pl.ds(128 * j, 128), :] = onehot(col == ((lane // 4) % 8) * 64 + j * 4 + lane % 4)
+        load_l.wait()
+        load_a.wait()
+        load_g.wait()
+
     acc[...] = jnp.zeros_like(acc)
-
-    pl.semaphore_wait(barrier, 15)
-    own = wg.at[c, z, x, h]
-    w_h = take()
-    send(wblk, own, w_h, {"dp": h_peer})
-    wg[c, z, x, h] = wblk[...]
-    load_a.wait()
-    load_g.wait()
 
     sel_r = iota((256, 128), 0)
     sel_c = iota((256, 128), 1)
@@ -175,38 +202,154 @@
                     )
                     xa = dot(a4, sel_a).astype(BF16)
                     xg = dot(g4, sel_g).astype(BF16)
-                    q = xx // 2
-                    off = pl.multiple_of(((xx % 2) * 2 + hh) * 128, 128)
                     for n in range(4):
-                        xs[cc, 2 * n + zl, q, 0:128, pl.ds(off, 128)] = xa[128 * n : 128 * n + 128]
-                        xs[cc, 2 * n + zl, q, 128:256, pl.ds(off, 128)] = xg[128 * n : 128 * n + 128]
+                        xs[cc, 2 * n + zl, xx, 0:128, 128 * hh : 128 * hh + 128] = xa[128 * n : 128 * n + 128]
+                        xs[cc, 2 * n + zl, xx, 128:256, 128 * hh : 128 * hh + 128] = xg[128 * n : 128 * n + 128]
             return carry
 
         lax.fori_loop(lo, hi, body, 0)
 
-    prepare(0, 2)
-    arrived(wg.at[c, z, x, 1 - h], w_h)
-    w_x = [take() for _ in range(3)]
-    for d in range(3):
-        send(wg.at[c, z, x], wg.at[c, z, x], w_x[d], {"dp": x_peers[d]})
-    prepare(2, 4)
-    for d in range(3):
-        arrived(wg.at[c, z, (x + 3 - d) % 4], w_x[d])
-
-    def multiply(color, zz, q):
-        w = wg[color, zz, pl.ds(2 * q, 2)]
-        wide = jnp.concatenate([w[0, 0], w[0, 1], w[1, 0], w[1, 1]], axis=1)
-        acc[...] += dot_nt(xs[color, zz, q], wide)
-
-    def project(s, mine, theirs):
-        if s == 0:
-            prepare(4, 8)
-        for zz, q in mine:
-            multiply(c, zz, q)
-        for zz, q in theirs:
-            multiply(1 - c, zz, q)
-
-    ring(lambda cc, zz, q: wg.at[cc, zz, pl.ds(2 * q, 2)], True, project)
+    def multiply_a(zz, x0, count):
+        for i in range(count):
+            w = jnp.concatenate([wa[zz, x0 + i, 0], wa[zz, x0 + i, 1]], axis=1)
+            acc[...] += dot_nt(xs[0, zz, x0 + i], w)
+
+    def multiply_b(xx):
+        def body(i, carry):
+            for zz in (2 * i, 2 * i + 1):
+                w = jnp.concatenate([wb[xx, 0, zz], wb[xx, 1, zz]], axis=1)
+                acc[...] += dot_nt(xs[1, zz, xx], w)
+            return carry
+
+        lax.fori_loop(0, 4, body, 0)
+
+    pl.semaphore_wait(barrier, 18)
+    hand_a = {("r", 0, 0): take(), ("r", 0, 1): take()}
+    pass_a = {}
+    for s in range(1, 5):
+        for kind, q in (("r", 0), ("l", 0), ("r", 1), ("l", 1)):
+            if s < 4 or (kind, q) in (("r", 0), ("l", 1)):
+                hand_a[(kind, s, q)] = take()
+                pass_a[(kind, s, q)] = take()
+    hand_b = {(n, q): take() for n in ("own", "left", "right", "far") for q in range(2)}
+    pass_b = {n: take() for n in ("r0", "r1", "l0", "l1", "far0", "far1")}
+    first = [take() for _ in range(15)]
+
+    def place(kind, s):
+        return (z + 8 - s) % 8 if kind == "r" else (z + s) % 8
+
+    def slot_a(zz, q):
+        return wa.at[zz, pl.ds(2 * q, 2)]
+
+    far = (x + 2) % 4
+    place_b = {"own": x, "left": (x + 3) % 4, "right": (x + 1) % 4, "far": far}
+    other = {"dp": c_peer}
+
+    @pl.when(c == 0)
+    def _():
+        base = len(sent)
+        ref = wa.at[z, x, h]
+        for i, peer in enumerate([h_peer] + x_peers):
+            send(ref, ref, first[i], {"dp": peer})
+        tables()
+        for d in range(3):
+            ref = wa.at[z, (x + 3 - d) % 4, h]
+            arrived(ref, first[1 + d])
+            send(ref, ref, first[4 + d], {"dp": h_peer})
+        prepare(0, 2)
+        arrived(wa.at[z, x, 1 - h], first[0])
+        for d in range(3):
+            arrived(wa.at[z, (x + 3 - d) % 4, 1 - h], first[4 + d])
+        right = {"dp": at((z + 1) % 8, x, h, c)}
+        left = {"dp": at((z + 7) % 8, x, h, c)}
+
+        def pass_on(kind, s, q):
+            ref = slot_a(place(kind, s - 1), q)
+            send(ref, ref, pass_a[(kind, s, q)], right if kind == "r" else left)
+
+        def hand(kind, s, q):
+            ref = slot_a(place(kind, s), q)
+            send(ref, ref, hand_a[(kind, s, q)], other)
+
+        for kind, q in (("r", 0), ("l", 1), ("r", 1), ("l", 0)):
+            pass_on(kind, 1, q)
+        hand("r", 0, 0)
+        hand("r", 0, 1)
+        prepare(2, 8)
+        todo = [(z, 0), (z, 1)]
+        for s in range(1, 5):
+            ready = []
+            for kind, q in (("r", 0), ("l", 1), ("r", 1), ("l", 0)):
+                if (kind, s, q) not in pass_a:
+                    continue
+                arrived(slot_a(place(kind, s), q), pass_a[(kind, s, q)])
+                if (kind, s + 1, q) in pass_a:
+                    pass_on(kind, s + 1, q)
+                hand(kind, s, q)
+                ready.append((place(kind, s), q))
+            for zz, q in todo:
+                multiply_a(zz, 2 * q, 2)
+            todo = ready
+        for zz, q in todo:
+            multiply_a(zz, 2 * q, 2)
+        for n in ("own", "left", "right", "far"):
+            for q in range(2):
+                arrived(wb.at[place_b[n], q], hand_b[(n, q)])
+            multiply_b(place_b[n])
+        for copy in sent[base:]:
+            copy.wait_send()
+        del sent[base:]
+
+    @pl.when(c == 1)
+    def _():
+        base = len(sent)
+        ref = wb.at[x, h, z]
+        for i, peer in enumerate([h_peer] + z_peers):
+            send(ref, ref, first[i], {"dp": peer})
+        tables()
+        for d in (0, 6, 1, 5, 2, 4, 3):
+            ref = wb.at[x, h, (z + 7 - d) % 8]
+            arrived(ref, first[1 + d])
+            send(ref, ref, first[8 + d], {"dp": h_peer})
+        prepare(0, 3)
+        arrived(wb.at[x, 1 - h, z], first[0])
+        for d in range(7):
+            arrived(wb.at[x, 1 - h, (z + 7 - d) % 8], first[8 + d])
+        right = {"dp": x_peers[0]}
+        left = {"dp": x_peers[2]}
+        for name, q, target in (("r0", 0, right), ("l1", 1, left), ("r1", 1, right), ("l0", 0, left)):
+            send(wb.at[x, q], wb.at[x, q], pass_b[name], target)
+        for q in range(2):
+            send(wb.at[x, q], wb.at[x, q], hand_b[("own", q)], other)
+        prepare(3, 8)
+        xl, xr = place_b["left"], place_b["right"]
+        arrived(wb.at[xl, 0], pass_b["r0"])
+        send(wb.at[xl, 0], wb.at[xl, 0], pass_b["far0"], right)
+        send(wb.at[xl, 0], wb.at[xl, 0], hand_b[("left", 0)], other)
+        arrived(wb.at[xr, 1], pass_b["l1"])
+        send(wb.at[xr, 1], wb.at[xr, 1], pass_b["far1"], left)
+        send(wb.at[xr, 1], wb.at[xr, 1], hand_b[("right", 1)], other)
+        multiply_b(x)
+        arrived(wb.at[xl, 1], pass_b["r1"])
+        send(wb.at[xl, 1], wb.at[xl, 1], hand_b[("left", 1)], other)
+        arrived(wb.at[xr, 0], pass_b["l0"])
+        send(wb.at[xr, 0], wb.at[xr, 0], hand_b[("right", 0)], other)
+        multiply_b(xl)
+        arrived(wb.at[far, 0], pass_b["far0"])
+        send(wb.at[far, 0], wb.at[far, 0], hand_b[("far", 0)], other)
+        arrived(wb.at[far, 1], pass_b["far1"])
+        send(wb.at[far, 1], wb.at[far, 1], hand_b[("far", 1)], other)
+        multiply_b(xr)
+        multiply_b(far)
+        for s in range(5):
+            for kind, q in (("r", 0), ("l", 1), ("r", 1), ("l", 0)):
+                if (kind, s, q) not in hand_a:
+                    continue
+                arrived(slot_a(place(kind, s), q), hand_a[(kind, s, q)])
+                multiply_a(place(kind, s), 2 * q, 2)
+        for copy in sent[base:]:
+            copy.wait_send()
+        del sent[base:]
 
     tok = iota((128, 64), 0)
     length = jnp.zeros((128, 64), jnp.int32)
@@ -276,18 +419,16 @@
     yc = iota((64, 256), 1)
     quarter = jnp.where(yc < 128, yc // 32, (yc // 4) % 4) == yr // 16
     spread = jnp.where(quarter, spread, 0.0)
-    lx[ly] = spread[0:16] + spread[16:32] + spread[32:48] + spread[48:64]
-
-    l_s = [take() for _ in range(3)]
-    for d in range(3):
-        send(lx.at[ly], lx.at[ly], l_s[d], {"layer": (ly + 1 + d) % 4})
-    for d in range(3):
-        arrived(lx.at[(ly + 3 - d) % 4], l_s[d])
-    kb[c, x, h] = (lx[0] + lx[1]) + (lx[2] + lx[3])
-
-    k_h = take()
-    send(kb.at[c, x, h], kb.at[c, x, h], k_h, {"dp": h_peer})
-    arrived(kb.at[c, x, 1 - h], k_h)
+    lx[h, ly] = spread[0:16] + spread[16:32] + spread[32:48] + spread[48:64]
+
+    l_s = [(d, hh, take()) for d in range(4) for hh in range(2) if d + hh > 0]
+    for d, hh, sem in l_s:
+        peer = {"dp": at(z, x, (h + hh) % 2, c), "layer": (ly + d) % 4}
+        send(lx.at[h, ly], lx.at[h, ly], sem, peer)
+    for d, hh, sem in l_s:
+        arrived(lx.at[(h + hh) % 2, (ly + 4 - d) % 4], sem)
+    for hh in range(2):
+        kb[c, x, hh] = (lx[hh, 0] + lx[hh, 1]) + (lx[hh, 2] + lx[hh, 3])
     k_x = [take() for _ in range(3)]
     k_c = [take() for _ in range(4)]
     for d in range(3):
@@ -326,56 +467,157 @@
         copy.wait_send()
 
 
-def run_front(act, grd, wblk, qblk, lens):
+def run_front(act, grd, inb, outb, qry, lens):
     vmem = pl.BlockSpec(memory_space=pltpu.VMEM)
-    hbm = pl.BlockSpec(memory_space=pl.ANY)
+    hbm = pl.BlockSpec(memory_space=pltpu.HBM)
     return pl.pallas_call(
         front,
         out_shape=(jax.ShapeDtypeStruct((128, 128), BF16), jax.ShapeDtypeStruct((8, 2, 32, 640), F32)),
-        in_specs=[hbm, hbm, vmem, vmem, pl.BlockSpec(memory_space=pltpu.SMEM)],
+        in_specs=[hbm] * 6,
         out_specs=(vmem, vmem),
         scratch_shapes=[
             pltpu.VMEM(act.shape, BF16),
             pltpu.VMEM(grd.shape, BF16),
-            pltpu.VMEM((2, 8, 2, 256, 512), BF16),
-            pltpu.VMEM((2, 8, 4, 2, 64, 128), BF16),
+            pltpu.VMEM(inb.shape, BF16),
+            pltpu.VMEM(outb.shape, BF16),
+            pltpu.VMEM(qry.shape, BF16),
+            pltpu.SMEM((1, 4), jnp.int32),
+            pltpu.VMEM((2, 8, 4, 256, 256), BF16),
+            pltpu.VMEM((8, 4, 2, 64, 128), BF16),
+            pltpu.VMEM((4, 2, 8, 64, 128), BF16),
             pltpu.VMEM((2, 4, 2, 128, 128), BF16),
             pltpu.VMEM((9, 128, 128), BF16),
-            pltpu.VMEM((4, 16, 256), F32),
+            pltpu.VMEM((2, 4, 16, 256), F32),
             pltpu.VMEM((2, 4, 2, 16, 256), F32),
             pltpu.VMEM((2048, 512), BF16),
             pltpu.VMEM((256, 64), F32),
-            pltpu.SemaphoreType.DMA((2,)),
+            pltpu.SemaphoreType.DMA((6,)),
             pltpu.SemaphoreType.DMA((SEMS,)),
             pltpu.SemaphoreType.DMA((SEMS,)),
         ],
         compiler_params=pltpu.CompilerParams(collective_id=0, has_side_effects=True, vmem_limit_bytes=48 * 1024 * 1024),
         name="front",
-    )(act, grd, wblk, qblk, lens)
-
-
-def solve(whole, query_index):
-    kernel = whole[:, :512]
-    inner = whole[:, 512:576]
-    pair_total = kernel.shape[0]
-    mean_diag = jnp.trace(kernel) / pair_total
+    )(*[pltpu.with_memory_space_constraint(v, pltpu.HBM) for v in (act, grd, inb, outb, qry, lens)])
+
+
+HIGH = lax.Precision.HIGHEST
+
+
+STRIP = 32
+
+
+def invert(d):
+    sub = iota((8, 128), 0)
+    lane = iota((8, 128), 1)
+    big_row = iota((128, 128), 0) // STRIP
+    big_col = iota((128, 128), 1) // STRIP
+    per = STRIP // 8
+    for s in range(128 // STRIP):
+        rows = [d[8 * i : 8 * i + 8, :] for i in range(s * per, s * per + per)]
+        for p in range(per):
+            first = s * STRIP + 8 * p
+            inside = lane // 8 == first // 8
+            head = rows[p]
+            cols = [jnp.broadcast_to(head[:, first + k : first + k + 1], (8, 128)) for k in range(8)]
+            head = jnp.where(inside, jnp.where(lane % 8 == sub, 1.0, 0.0), head)
+            for k in range(8):
+                here = sub == k
+                f = cols[k]
+                pivot = 1.0 / f[k : k + 1, :]
+                lead = head[k : k + 1, :] * pivot
+                head = jnp.where(here, lead, head - f * lead)
+                for j in range(k + 1, 8):
+                    g = cols[j][k : k + 1, :] * pivot
+                    cols[j] = jnp.where(here, g, cols[j] - f * g)
+            leads = [jnp.broadcast_to(head[k : k + 1, :], (8, 128)) for k in range(8)]
+            for i in range(per):
+                if i == p:
+                    continue
+                v = rows[i]
+                r = jnp.where(inside, 0.0, v)
+                for k in range(8):
+                    r = r - v[:, first + k : first + k + 1] * leads[k]
+                rows[i] = r
+            rows[p] = head
+        done = jnp.concatenate(rows, axis=0)
+        zero = jnp.zeros((STRIP, 128), F32)
+        placed = jnp.concatenate([done if t == s else zero for t in range(128 // STRIP)], axis=0)
+        side = jnp.where((big_col == s) & (big_row != s), d, 0.0)
+        keep = jnp.where(big_col == s, 0.0, d)
+        keep = jnp.where(big_row == s, placed, keep)
+        d = keep - jnp.dot(side, placed, precision=HIGH, preferred_element_type=F32)
+    return d
+
+
+def solver(sk, whole, qidx_hbm, sketch, scores, a, qidx, sem):
+    load = pltpu.make_async_copy(qidx_hbm, qidx, sem)
+    load.start()
+    flat = sk[...].astype(F32)
+    for m in range(32):
+        sketch[:, 128 * m : 128 * m + 128] = flat[4 * m : 4 * m + 4].astype(BF16)
+    a[...] = whole[...]
+    row = iota((128, 128), 0)
+    col = iota((128, 128), 1)
+    diag = jnp.zeros((128, 128), F32)
+    for j in range(4):
+        diag = diag + jnp.where(row == col, whole[128 * j : 128 * j + 128, 128 * j : 128 * j + 128], 0.0)
+    mean_diag = jnp.sum(diag) / 512.0
     damping = damp_ratio * mean_diag
-    factor = jnp.linalg.cholesky(kernel + damping * jnp.eye(pair_total, dtype=F32))
-    solved = jax.scipy.linalg.cho_solve((factor, True), inner)
-    own_rows = lax.dynamic_slice_in_dim(solved, lax.axis_index("dp") * 4, 4, 0)
-    selected = query_index[:, :, None] == jnp.arange(64, dtype=jnp.int32)[None, None, :]
-    picked = jnp.sum(jnp.where(selected, own_rows[:, None, :], jnp.float32(0.0)), axis=-1)
-    return jnp.sqrt(mean_diag) * picked
+
+    def step(j, carry):
+        at = pl.multiple_of(j * 128, 128)
+        block = a[pl.ds(at, 128), pl.ds(at, 128)] + jnp.where(row == col, damping, 0.0)
+        inv = invert(block)
+        for n in range(4):
+
+            @pl.when(j == n)
+            def _():
+                lo = 128 * n
+                hi = lo + 128
+                lead = jnp.dot(inv, a[lo:hi, hi:640], precision=HIGH, preferred_element_type=F32)
+                a[lo:hi, hi:640] = lead
+                if n < 3:
+                    a[hi:512, hi:640] -= jnp.dot(a[hi:512, lo:hi], lead, precision=HIGH, preferred_element_type=F32)
+
+        return carry
+
+    lax.fori_loop(0, 4, step, 0)
+    for n in range(2, -1, -1):
+        lo = 128 * n
+        hi = lo + 128
+        a[lo:hi, 512:640] -= jnp.dot(a[lo:hi, hi:512], a[hi:512, 512:640], precision=HIGH, preferred_element_type=F32)
+    me = lax.axis_index("dp")
+    pick = jnp.where(iota((8, 512), 1) == me * 4 + iota((8, 512), 0), 1.0, 0.0).astype(F32)
+    own = jnp.dot(pick, a[:, 512:640], precision=HIGH, preferred_element_type=F32)[0:4]
+    load.wait()
+    lanes = iota((4, 128), 1)
+    spot = iota((4, 8), 1)
+    out = jnp.zeros((4, 8), F32)
+    for s in range(8):
+        chosen = jnp.sum(jnp.where(lanes == qidx[:, s : s + 1], own, 0.0), axis=1, keepdims=True)
+        out = jnp.where(spot == s, chosen, out)
+    scores[...] = jnp.sqrt(mean_diag) * out
+
+
+def solve(sk, whole, query_index):
+    vmem = pl.BlockSpec(memory_space=pltpu.VMEM)
+    return pl.pallas_call(
+        solver,
+        out_shape=(jax.ShapeDtypeStruct((4, 4096), BF16), jax.ShapeDtypeStruct((4, 8), F32)),
+        in_specs=[vmem, vmem, pl.BlockSpec(memory_space=pltpu.HBM)],
+        out_specs=(vmem, vmem),
+        scratch_shapes=[pltpu.VMEM((512, 640), F32), pltpu.VMEM((4, 8), jnp.int32), pltpu.SemaphoreType.DMA],
+        compiler_params=pltpu.CompilerParams(vmem_limit_bytes=32 * 1024 * 1024),
+        name="solver",
+    )(sk, whole, pltpu.with_memory_space_constraint(query_index, pltpu.HBM))
 
 
 def local(activations, out_grads, in_basis, out_basis, queries, pair_lengths, query_index):
-    wblk = jnp.concatenate([in_basis[0].T, out_basis[0].T, jnp.zeros((64, 24), BF16)], axis=1)
-    first = (lax.axis_index("dp") % 16) * 4
-    qrows = lax.dynamic_slice_in_dim(queries[0], first, 4, 0)
-    qblk = qrows.reshape(4, 32, 128).transpose(1, 0, 2).reshape(128, 128)
-    sk, kin = run_front(activations[0], out_grads[0], wblk, qblk, pair_lengths)
-    sketch = sk.reshape(32, 4, 128).transpose(1, 0, 2).reshape(1, 4, 4096)
-    return sketch, solve(kin.reshape(512, 640), query_index)
+    sk, kin = run_front(
+        activations[0], out_grads[0], in_basis[0].T, out_basis[0], queries[0], pair_lengths
+    )
+    sketch, scores = solve(sk, kin.reshape(512, 640), query_index)
+    return sketch[None], scores
 
 
 def solution(mesh):

time: 255 us -> 108 us (0.42); the launches traced: 251 us -> 108 us
  other arithmetic: 124 us -> 0 us
  local copies, waits for them, and re-layouts: 24.4 us -> 0 us
  Pallas kernels: 86.3 us -> 107 us
  matrix products: 11.2 us -> 0 us
  between operations: 5.25 us -> 0.8 us
    another operation x18 -> x0, other arithmetic: 119 us -> none  [the longest x14 78.7 us: solve(): jnp.linalg.cholesky(kernel + damping * jnp.eye(pair_total, dtype=F32))]
    pallas_call x0 -> x1, Pallas kernels: none -> 21.9 us  [solve(): pl.pallas_call(solver, out_shape=(jax.ShapeDtypeStruct((4, 4096), BF16),...]
    another operation x35 -> x0, local copies, waits for them, and re-layouts: 12.7 us -> none
    another operation x20 -> x0, matrix products: 11.2 us -> none  [the longest x6 6.09 us: solve(): jnp.linalg.cholesky(kernel + damping * jnp.eye(pair_total, dtype=F32))]
    unnamed x20 -> x0, local copies, waits for them, and re-layouts: 7.79 us -> none
    add x1 -> x0, local copies, waits for them, and re-layouts: 2.59 us -> none  [solve(): kernel + damping * jnp.eye(pair_total, dtype=F32)]
where the time goes in v2:
time: 108 us
  Pallas kernels  107 us (99%)
    pallas_call x1, Pallas kernels, run_front(): pl.pallas_call(front, out_shape=(jax.ShapeDtypeStruct((128, 128), BF16),...  84.9 us
    pallas_call x1, Pallas kernels, solve(): pl.pallas_call(solver, out_shape=(jax.ShapeDtypeStruct((4, 4096), BF16),...  21.9 us

profile of v2, /device:TPU:1, one launch (start us, length us, event | category | flops | bytes accessed | tf_op | source)
XLA Modules:
  0.0 107.6 jit_solution(12620710496782126639)
XLA Ops:
  0.6 84.9 %front.1 = (bf16[128,128]{1,0:T(8,128)(2,1)S(1)}, f32[8,2,32,640]{3,2,1,0:T(8,128)S(1)}) custom-call(bf16[128,9728]{1,0:T(8,128)(2,1)} %bitcast.10, bf16[128,3584]{1,0:T(8,128)(2,1)} %bitcast.11, bf16[64,76]{1,0:T(8,128)(2,1)} %bitcast.13, bf16[28,64]{1,0:T(8,128)(2,1)} %bitcast.14, bf16[64,4096]{1,0:T(8,128)(2,1)} %bitcast.12, s32[1,4]{1,0:T(1,128)} %lens_hbm.1), custom_call_target="tpu_custom_call" | custom-call | tf_op jit(solution)/shard_map/front/pallas_call | solution.py:473
  85.5 21.9 %solver.1 = (bf16[4,4096]{1,0:T(4,128)(2,1)}, f32[4,8]{1,0:T(4,128)}) custom-call(bf16[128,128]{1,0:T(8,128)(2,1)S(1)} %get-tuple-element.6.sk, f32[512,640]{1,0:T(8,128)S(1)} %bitcast.9, s32[4,8]{1,0:T(4,128)} %qidx_hbm.1), custom_call_target="tpu_custom_call" | custom-call | tf_op jit(solution)/shard_map/solver/pallas_call | solution.py:604

commit v3 on v2

--- a/solution.py
+++ b/solution.py
@@ -10,7 +10,7 @@
 F32 = jnp.float32
 BF16 = jnp.bfloat16
 NT = (((1,), (1,)), ((), ()))
-SEMS = 160
+SEMS = 192
 
 
 def iota(shape, dim):
@@ -36,7 +36,73 @@
     return lax.dot_general(a, b, NT, preferred_element_type=F32)
 
 
-def front(act, grd, inb_hbm, outb_hbm, qry_hbm, lens_hbm, sk, kin, av, gv, inb, outb, qry, lens, xs, wa, wb, srow, scol, lx, kb, perm, acc, in_sem, ssem, rsem):
+HIGH = lax.Precision.HIGHEST
+
+
+STRIP = 64
+PANEL = 16
+PV = 2
+
+
+def invert(d, between):
+    sub = iota((8, 128), 0)
+    lane = iota((8, 128), 1)
+    big_row = iota((STRIP, 128), 0)
+    big_col = iota((STRIP, 128), 1) // STRIP
+    per = STRIP // 8
+    count = 128 // STRIP
+    strips = [d[STRIP * s : STRIP * s + STRIP, :] for s in range(count)]
+    for s in range(count):
+        rows = [strips[s][8 * i : 8 * i + 8, :] for i in range(per)]
+        for p in range(0, per, PV):
+            first = s * STRIP + 8 * p
+            inside = lane // PANEL == first // PANEL
+            heads = rows[p : p + PV]
+            cols = [[jnp.broadcast_to(v[:, first + k : first + k + 1], (8, 128)) for v in heads] for k in range(PANEL)]
+            heads = [
+                jnp.where(inside, jnp.where(lane % PANEL == sub + 8 * n, 1.0, 0.0), v) for n, v in enumerate(heads)
+            ]
+            for k in range(PANEL):
+                n0, r0 = k // 8, k % 8
+                here = sub == r0
+                f = cols[k]
+                pivot = 1.0 / f[n0][r0 : r0 + 1, :]
+                for j in range(k + 1, PANEL):
+                    g = cols[j][n0][r0 : r0 + 1, :] * pivot
+                    cols[j] = [
+                        jnp.where(here, g, v - f[n] * g) if n == n0 else v - f[n] * g for n, v in enumerate(cols[j])
+                    ]
+                lead = heads[n0][r0 : r0 + 1, :] * pivot
+                heads = [
+                    jnp.where(here, lead, v - f[n] * lead) if n == n0 else v - f[n] * lead for n, v in enumerate(heads)
+                ]
+            rows[p : p + PV] = heads
+            others = [i for i in range(per) if not p <= i < p + PV]
+            if others:
+                leads = [jnp.broadcast_to(heads[k // 8][k % 8 : k % 8 + 1, :], (8, 128)) for k in range(PANEL)]
+                for i in others:
+                    v = rows[i]
+                    r = jnp.where(inside, 0.0, v)
+                    for k in range(PANEL):
+                        r = r - v[:, first + k : first + k + 1] * leads[k]
+                    rows[i] = r
+        done = jnp.concatenate(rows, axis=0) if per > 1 else rows[0]
+        zero = jnp.zeros((STRIP, 128), F32)
+        placed = jnp.concatenate([done if t == s else zero for t in range(count)], axis=0)
+        new = [None] * count
+        new[s] = done
+        for t in [(s + i) % count for i in range(1, count)]:
+            v = strips[t]
+            side = jnp.where(big_col == s, v, 0.0)
+            keep = jnp.where(big_col == s, 0.0, v)
+            new[t] = keep - jnp.dot(side, placed, precision=HIGH, preferred_element_type=F32)
+        strips = new
+        if s == 0:
+            between()
+    return jnp.concatenate(strips, axis=0)
+
+
+def front(act, grd, inb_hbm, outb_hbm, qry_hbm, lens_hbm, qidx_hbm, sk, scores, kin, a, tz, tl, qidx, av, gv, inb, outb, qry, lens, xs, wa, wb, srow, scol, lx, kb, perm, acc, in_sem, ssem, rsem):
     me = lax.axis_index("dp")
     ly = lax.axis_index("layer")
     c = me % 2
@@ -59,7 +125,8 @@
     load_i = pltpu.make_async_copy(inb_hbm, inb, in_sem.at[3])
     load_o = pltpu.make_async_copy(outb_hbm, outb, in_sem.at[4])
     load_q = pltpu.make_async_copy(qry_hbm, qry, in_sem.at[5])
-    for load in (load_i, load_o, load_a, load_g, load_q, load_l):
+    load_x = pltpu.make_async_copy(qidx_hbm, qidx, in_sem.at[6])
+    for load in (load_i, load_o, load_a, load_g, load_q, load_l, load_x):
         load.start()
 
     barrier = pltpu.get_barrier_semaphore()
@@ -88,59 +155,6 @@
         pltpu.make_async_remote_copy(
             src_ref=slot, dst_ref=slot, send_sem=ssem.at[sem], recv_sem=rsem.at[sem], device_id={"dp": c_peer}, device_id_type=MESH
         ).wait_recv()
-
-    def ring(slot, forward_own, step_work):
-        right = {"dp": at((z + 1) % 8, x, h, c)}
-        left = {"dp": at((z + 7) % 8, x, h, c)}
-        other = {"dp": c_peer}
-        names = {}
-
-        def name(kind, s, q):
-            if (kind, s, q) not in names:
-                names[(kind, s, q)] = take()
-            return names[(kind, s, q)]
-
-        def goes(kind, s, q):
-            return s < 4 or (kind == "r" and q == 0) or (kind == "l" and q == 1)
-
-        def place(kind, s):
-            return (z + 8 - s) % 8 if kind == "r" else (z + s) % 8
-
-        def pass_on(kind, s, q):
-            target = right if kind == "r" else left
-            ref = slot(c, place(kind, s - 1), q)
-            send(ref, ref, name(kind, s, q), target)
-
-        def hand(kind, s, q):
-            ref = slot(c, place(kind, s), q)
-            send(ref, ref, name("f" + kind, s, q), other)
-
-        for q in range(2):
-            pass_on("r", 1, q)
-            pass_on("l", 1, q)
-        if forward_own:
-            for q in range(2):
-                hand("r", 0, q)
-        step_work(0, [(z, 0), (z, 1)], [])
-        pending = [("r", 0, 0), ("r", 0, 1)] if forward_own else []
-        for s in range(1, 5):
-            got = []
-            for q in range(2):
-                for kind in ("r", "l"):
-                    if not goes(kind, s, q):
-                        continue
-                    arrived(slot(c, place(kind, s), q), name(kind, s, q))
-                    if s < 4 and goes(kind, s + 1, q):
-                        pass_on(kind, s + 1, q)
-                    hand(kind, s, q)
-                    got.append((kind, s, q))
-            for kind, t, q in pending:
-                arrived(slot(1 - c, place(kind, t), q), name("f" + kind, t, q))
-            step_work(s, [(place(k, t), q) for k, t, q in got], [(place(k, t), q) for k, t, q in pending])
-            pending = got
-        for kind, t, q in pending:
-            arrived(slot(1 - c, place(kind, t), q), name("f" + kind, t, q))
-        step_work(5, [], [(place(k, t), q) for k, t, q in pending])
 
     eye = onehot(iota((64, 64), 0) == iota((64, 64), 1))
     load_i.wait()
@@ -372,7 +386,8 @@
         rights = dot(right_proj, onehot(j_col == j_row + 64 * par)).astype(BF16)
         total = total + dot(lefts, rights)
     sketch = total.astype(BF16)
-    sk[...] = sketch
+    for m in range(32):
+        sk[:, 128 * m : 128 * m + 128] = total[4 * m : 4 * m + 4].astype(BF16)
     srow[c, x, h] = sketch
     scol[z] = sketch
 
@@ -396,6 +411,15 @@
     for d in range(4):
         arrived(srow.at[1 - c, (x + 4 - d) % 4], s_c[d])
 
+    squares = jnp.zeros((8, 128), F32)
+    for cc in range(2):
+        for xx in range(4):
+            v = srow[cc, xx].astype(F32)
+            squares = squares + jnp.sum((v * v).reshape(32, 8, 128), axis=0)
+    tz[z] = squares
+    t_z = [take() for _ in range(7)]
+    for d in range(7):
+        send(tz.at[z], tz.at[z], t_z[d], {"dp": z_peers[d]})
     gram = jnp.zeros((256, 144), F32)
     for u in range(4):
         rows = [srow[:, :, :, pl.ds(32 * u + 16 * v, 16), :].reshape(256, 128) for v in range(2)]
@@ -429,6 +453,15 @@
         arrived(lx.at[(h + hh) % 2, (ly + 4 - d) % 4], sem)
     for hh in range(2):
         kb[c, x, hh] = (lx[hh, 0] + lx[hh, 1]) + (lx[hh, 2] + lx[hh, 3])
+    for d in range(7):
+        arrived(tz.at[(z + 7 - d) % 8], t_z[d])
+    plane_sums = tz[0]
+    for n in range(1, 8):
+        plane_sums = plane_sums + tz[n]
+    tl[ly] = plane_sums
+    t_l = [take() for _ in range(3)]
+    for d in range(3):
+        send(tl.at[ly], tl.at[ly], t_l[d], {"layer": (ly + 1 + d) % 4})
     k_x = [take() for _ in range(3)]
     k_c = [take() for _ in range(4)]
     for d in range(3):
@@ -459,23 +492,95 @@
     ic = iota((256, 128), 1)
     place_q = onehot(ic == (ir // 16) * 4 + ir % 4)
     part_q = sum(dot(v, place_q) for v in pieces(sides))
-    for cc in range(2):
-        kin[z, cc, :, 0:512] = part[32 * cc : 32 * cc + 32]
-        kin[z, cc, :, 512:640] = part_q[32 * cc : 32 * cc + 32]
-    ring(lambda cc, zz, q: kin.at[zz, cc, pl.ds(16 * q, 16)], False, lambda s, mine, theirs: None)
+    kin[pl.ds(pl.multiple_of(64 * z, 64), 64), 0:512] = part
+    kin[pl.ds(pl.multiple_of(64 * z, 64), 64), 512:640] = part_q
+    for d in range(3):
+        arrived(tl.at[(ly + 3 - d) % 4], t_l[d])
+    mean_diag = jnp.sum((tl[0] + tl[1]) + (tl[2] + tl[3])) / 512.0
+    damping = damp_ratio * mean_diag
+    ring = {}
+    for s in range(1, 5):
+        for kind, q in (("r", 0), ("l", 1), ("r", 1), ("l", 0)):
+            if s < 4 or (kind, q) in (("r", 0), ("l", 1)):
+                ring[(kind, s, q)] = (take(), take())
+    right = {"dp": at((z + 1) % 8, x, h, c)}
+    left = {"dp": at((z + 7) % 8, x, h, c)}
+
+    def rows_at(cc, zz, q):
+        return kin.at[pl.ds(pl.multiple_of(64 * zz + 32 * cc + 16 * q, 16), 16)]
+
+    def pass_rows(kind, s, q):
+        ref = rows_at(c, place(kind, s - 1), q)
+        send(ref, ref, ring[(kind, s, q)][0], right if kind == "r" else left)
+
+    swing = 2 * (z % 2) - 1
+    home = z // 2
+    order = [home, (home + 4 + swing) % 4, (home + 4 - swing) % 4, (home + 2) % 4]
+    spans = [pl.ds(pl.multiple_of(128 * i, 128), 128) for i in order]
+    here = iota((128, 640), 0)
+    there = iota((128, 640), 1)
+
+    def eliminate(t):
+        a[t] = kin[spans[t], :] + jnp.where(there == here + 128 * order[t], damping, 0.0)
+        for n in range(t):
+            a[t] = a[t] - jnp.dot(a[t, :, spans[n]], a[n], precision=HIGH, preferred_element_type=F32)
+        inv = invert(a[t, :, spans[t]], lambda: take_hop(t + 2))
+        a[t] = jnp.dot(inv, a[t], precision=HIGH, preferred_element_type=F32)
+
+    for kind, q in (("r", 0), ("l", 1), ("r", 1), ("l", 0)):
+        pass_rows(kind, 1, q)
+    def take_hop(s):
+        for kind, _, q in [n for n in ring if n[1] == s]:
+            ref = rows_at(c, place(kind, s), q)
+            arrived(ref, ring[(kind, s, q)][0])
+            if (kind, s + 1, q) in ring:
+                pass_rows(kind, s + 1, q)
+            send(ref, ref, ring[(kind, s, q)][1], other)
+
+    take_hop(1)
+    for s in range(1, 5):
+        for kind, _, q in [n for n in ring if n[1] == s]:
+            arrived(rows_at(1 - c, place(kind, s), q), ring[(kind, s, q)][1])
+        eliminate(s - 1)
+
+    def apply(left_rows, n, value):
+        return jnp.dot(left_rows(spans[n]), value, precision=HIGH, preferred_element_type=F32)
+
+    x3 = a[3, :, 512:640]
+    x2 = a[2, :, 512:640] - apply(lambda at_: a[2, :, at_], 3, x3)
+    x1 = a[1, :, 512:640] - apply(lambda at_: a[1, :, at_], 3, x3) - apply(lambda at_: a[1, :, at_], 2, x2)
+    pick = jnp.where(iota((8, 128), 1) == (me * 4 - 128 * home) + iota((8, 128), 0), 1.0, 0.0).astype(F32)
+    own_x = jnp.dot(pick, a[0, :, 512:640], precision=HIGH, preferred_element_type=F32)
+    for n, value in ((3, x3), (2, x2), (1, x1)):
+        coef = jnp.dot(pick, a[0, :, spans[n]], precision=HIGH, preferred_element_type=F32)
+        own_x = own_x - jnp.dot(coef, value, precision=HIGH, preferred_element_type=F32)
+    own_x = own_x[0:4]
+    load_x.wait()
+    lanes = iota((4, 128), 1)
+    spot = iota((4, 8), 1)
+    out = jnp.zeros((4, 8), F32)
+    for n in range(8):
+        chosen = jnp.sum(jnp.where(lanes == qidx[:, n : n + 1], own_x, 0.0), axis=1, keepdims=True)
+        out = jnp.where(spot == n, chosen, out)
+    scores[...] = jnp.sqrt(mean_diag) * out
     for copy in sent:
         copy.wait_send()
 
 
-def run_front(act, grd, inb, outb, qry, lens):
+def run_front(act, grd, inb, outb, qry, lens, qidx):
     vmem = pl.BlockSpec(memory_space=pltpu.VMEM)
     hbm = pl.BlockSpec(memory_space=pltpu.HBM)
     return pl.pallas_call(
         front,
-        out_shape=(jax.ShapeDtypeStruct((128, 128), BF16), jax.ShapeDtypeStruct((8, 2, 32, 640), F32)),
-        in_specs=[hbm] * 6,
+        out_shape=(jax.ShapeDtypeStruct((4, 4096), BF16), jax.ShapeDtypeStruct((4, 8), F32)),
+        in_specs=[hbm] * 7,
         out_specs=(vmem, vmem),
         scratch_shapes=[
+            pltpu.VMEM((512, 640), F32),
+            pltpu.VMEM((4, 128, 640), F32),
+            pltpu.VMEM((8, 8, 128), F32),
+            pltpu.VMEM((4, 8, 128), F32),
+            pltpu.VMEM((4, 8), jnp.int32),
             pltpu.VMEM(act.shape, BF16),
             pltpu.VMEM(grd.shape, BF16),
             pltpu.VMEM(inb.shape, BF16),
@@ -491,132 +596,19 @@
             pltpu.VMEM((2, 4, 2, 16, 256), F32),
             pltpu.VMEM((2048, 512), BF16),
             pltpu.VMEM((256, 64), F32),
-            pltpu.SemaphoreType.DMA((6,)),
+            pltpu.SemaphoreType.DMA((7,)),
             pltpu.SemaphoreType.DMA((SEMS,)),
             pltpu.SemaphoreType.DMA((SEMS,)),
         ],
         compiler_params=pltpu.CompilerParams(collective_id=0, has_side_effects=True, vmem_limit_bytes=48 * 1024 * 1024),
         name="front",
-    )(*[pltpu.with_memory_space_constraint(v, pltpu.HBM) for v in (act, grd, inb, outb, qry, lens)])
-
-
-HIGH = lax.Precision.HIGHEST
-
-
-STRIP = 32
-
-
-def invert(d):
-    sub = iota((8, 128), 0)
-    lane = iota((8, 128), 1)
-    big_row = iota((128, 128), 0) // STRIP
-    big_col = iota((128, 128), 1) // STRIP
-    per = STRIP // 8
-    for s in range(128 // STRIP):
-        rows = [d[8 * i : 8 * i + 8, :] for i in range(s * per, s * per + per)]
-        for p in range(per):
-            first = s * STRIP + 8 * p
-            inside = lane // 8 == first // 8
-            head = rows[p]
-            cols = [jnp.broadcast_to(head[:, first + k : first + k + 1], (8, 128)) for k in range(8)]
-            head = jnp.where(inside, jnp.where(lane % 8 == sub, 1.0, 0.0), head)
-            for k in range(8):
-                here = sub == k
-                f = cols[k]
-                pivot = 1.0 / f[k : k + 1, :]
-                lead = head[k : k + 1, :] * pivot
-                head = jnp.where(here, lead, head - f * lead)
-                for j in range(k + 1, 8):
-                    g = cols[j][k : k + 1, :] * pivot
-                    cols[j] = jnp.where(here, g, cols[j] - f * g)
-            leads = [jnp.broadcast_to(head[k : k + 1, :], (8, 128)) for k in range(8)]
-            for i in range(per):
-                if i == p:
-                    continue
-                v = rows[i]
-                r = jnp.where(inside, 0.0, v)
-                for k in range(8):
-                    r = r - v[:, first + k : first + k + 1] * leads[k]
-                rows[i] = r
-            rows[p] = head
-        done = jnp.concatenate(rows, axis=0)
-        zero = jnp.zeros((STRIP, 128), F32)
-        placed = jnp.concatenate([done if t == s else zero for t in range(128 // STRIP)], axis=0)
-        side = jnp.where((big_col == s) & (big_row != s), d, 0.0)
-        keep = jnp.where(big_col == s, 0.0, d)
-        keep = jnp.where(big_row == s, placed, keep)
-        d = keep - jnp.dot(side, placed, precision=HIGH, preferred_element_type=F32)
-    return d
-
-
-def solver(sk, whole, qidx_hbm, sketch, scores, a, qidx, sem):
-    load = pltpu.make_async_copy(qidx_hbm, qidx, sem)
-    load.start()
-    flat = sk[...].astype(F32)
-    for m in range(32):
-        sketch[:, 128 * m : 128 * m + 128] = flat[4 * m : 4 * m + 4].astype(BF16)
-    a[...] = whole[...]
-    row = iota((128, 128), 0)
-    col = iota((128, 128), 1)
-    diag = jnp.zeros((128, 128), F32)
-    for j in range(4):
-        diag = diag + jnp.where(row == col, whole[128 * j : 128 * j + 128, 128 * j : 128 * j + 128], 0.0)
-    mean_diag = jnp.sum(diag) / 512.0
-    damping = damp_ratio * mean_diag
-
-    def step(j, carry):
-        at = pl.multiple_of(j * 128, 128)
-        block = a[pl.ds(at, 128), pl.ds(at, 128)] + jnp.where(row == col, damping, 0.0)
-        inv = invert(block)
-        for n in range(4):
-
-            @pl.when(j == n)
-            def _():
-                lo = 128 * n
-                hi = lo + 128
-                lead = jnp.dot(inv, a[lo:hi, hi:640], precision=HIGH, preferred_element_type=F32)
-                a[lo:hi, hi:640] = lead
-                if n < 3:
-                    a[hi:512, hi:640] -= jnp.dot(a[hi:512, lo:hi], lead, precision=HIGH, preferred_element_type=F32)
-
-        return carry
-
-    lax.fori_loop(0, 4, step, 0)
-    for n in range(2, -1, -1):
-        lo = 128 * n
-        hi = lo + 128
-        a[lo:hi, 512:640] -= jnp.dot(a[lo:hi, hi:512], a[hi:512, 512:640], precision=HIGH, preferred_element_type=F32)
-    me = lax.axis_index("dp")
-    pick = jnp.where(iota((8, 512), 1) == me * 4 + iota((8, 512), 0), 1.0, 0.0).astype(F32)
-    own = jnp.dot(pick, a[:, 512:640], precision=HIGH, preferred_element_type=F32)[0:4]
-    load.wait()
-    lanes = iota((4, 128), 1)
-    spot = iota((4, 8), 1)
-    out = jnp.zeros((4, 8), F32)
-    for s in range(8):
-        chosen = jnp.sum(jnp.where(lanes == qidx[:, s : s + 1], own, 0.0), axis=1, keepdims=True)
-        out = jnp.where(spot == s, chosen, out)
-    scores[...] = jnp.sqrt(mean_diag) * out
-
-
-def solve(sk, whole, query_index):
-    vmem = pl.BlockSpec(memory_space=pltpu.VMEM)
-    return pl.pallas_call(
-        solver,
-        out_shape=(jax.ShapeDtypeStruct((4, 4096), BF16), jax.ShapeDtypeStruct((4, 8), F32)),
-        in_specs=[vmem, vmem, pl.BlockSpec(memory_space=pltpu.HBM)],
-        out_specs=(vmem, vmem),
-        scratch_shapes=[pltpu.VMEM((512, 640), F32), pltpu.VMEM((4, 8), jnp.int32), pltpu.SemaphoreType.DMA],
-        compiler_params=pltpu.CompilerParams(vmem_limit_bytes=32 * 1024 * 1024),
-        name="solver",
-    )(sk, whole, pltpu.with_memory_space_constraint(query_index, pltpu.HBM))
+    )(*[pltpu.with_memory_space_constraint(v, pltpu.HBM) for v in (act, grd, inb, outb, qry, lens, qidx)])
 
 
 def local(activations, out_grads, in_basis, out_basis, queries, pair_lengths, query_index):
-    sk, kin = run_front(
-        activations[0], out_grads[0], in_basis[0].T, out_basis[0], queries[0], pair_lengths
+    sketch, scores = run_front(
+        activations[0], out_grads[0], in_basis[0].T, out_basis[0], queries[0], pair_lengths, query_index
     )
-    sketch, scores = solve(sk, kin.reshape(512, 640), query_index)
     return sketch[None], scores
 
 

time: 108 us -> 98.2 us (0.909)
  Pallas kernels: 107 us -> 96.1 us
  local copies, waits for them, and re-layouts: 0 us -> 1.19 us
    pallas_call x2 -> x1, Pallas kernels: 107 us -> 96.1 us  [run_front(): pl.pallas_call(front, out_shape=(jax.ShapeDtypeStruct((4, 4096), BF16), j...]
    unnamed x0 -> x2, local copies, waits for them, and re-layouts: none -> 1.19 us
where the time goes in v3:
time: 98.2 us; the launch traced here: 98 us
  Pallas kernels  96.1 us (98%)
  local copies, waits for them, and re-layouts  1.19 us (1%)
    pallas_call x1, Pallas kernels, run_front(): pl.pallas_call(front, out_shape=(jax.ShapeDtypeStruct((4, 4096), BF16), j...  96.1 us

profile of v3, /device:TPU:1, one launch (start us, length us, event | category | flops | bytes accessed | tf_op | source)
XLA Modules:
  0.0 98.0 jit_solution(5767888689612477981)
XLA Ops:
  0.6 96.1 %front.1 = (bf16[4,4096]{1,0:T(4,128)(2,1)S(1)}, f32[4,8]{1,0:T(4,128)S(1)}) custom-call(bf16[128,9728]{1,0:T(8,128)(2,1)} %bitcast.9, bf16[128,3584]{1,0:T(8,128)(2,1)} %bitcast.10, bf16[64,76]{1,0:T(8,128)(2,1)} %bitcast.12, bf16[28,64]{1,0:T(8,128)(2,1)} %bitcast.13, bf16[64,4096]{1,0:T(8,128)(2,1)} %bitcast.11, s32[1,4]{1,0:T(1,128)} %lens_hbm.1, ...), custom_call_target="tpu_custom_call" | custom-call | tf_op jit(solution)/shard_map/front/pallas_call | solution.py:573
  96.8 0.6 copy.11
  97.4 0.6 copy.12

commit v4 on v3

--- a/solution.py
+++ b/solution.py
@@ -166,7 +166,7 @@
 
     @pl.when(c == 0)
     def _():
-        wa[z, x, h] = own
+        wa[z, h, x] = own
 
     @pl.when(c == 1)
     def _():
@@ -187,6 +187,7 @@
         for j in range(16):
             perm[pl.ds(128 * j, 128), :] = onehot(col == ((lane // 4) % 8) * 64 + j * 4 + lane % 4)
         load_l.wait()
+        load_x.wait()
         load_a.wait()
         load_g.wait()
 
@@ -223,10 +224,10 @@
 
         lax.fori_loop(lo, hi, body, 0)
 
-    def multiply_a(zz, x0, count):
-        for i in range(count):
-            w = jnp.concatenate([wa[zz, x0 + i, 0], wa[zz, x0 + i, 1]], axis=1)
-            acc[...] += dot_nt(xs[0, zz, x0 + i], w)
+    def multiply_a(zz):
+        for i in range(4):
+            w = jnp.concatenate([wa[zz, 0, i], wa[zz, 1, i]], axis=1)
+            acc[...] += dot_nt(xs[0, zz, i], w)
 
     def multiply_b(xx):
         def body(i, carry):
@@ -253,7 +254,7 @@
         return (z + 8 - s) % 8 if kind == "r" else (z + s) % 8
 
     def slot_a(zz, q):
-        return wa.at[zz, pl.ds(2 * q, 2)]
+        return wa.at[zz, (h + q) % 2]
 
     far = (x + 2) % 4
     place_b = {"own": x, "left": (x + 3) % 4, "right": (x + 1) % 4, "far": far}
@@ -262,18 +263,10 @@
     @pl.when(c == 0)
     def _():
         base = len(sent)
-        ref = wa.at[z, x, h]
+        ref = wa.at[z, h, x]
         for i, peer in enumerate([h_peer] + x_peers):
             send(ref, ref, first[i], {"dp": peer})
         tables()
-        for d in range(3):
-            ref = wa.at[z, (x + 3 - d) % 4, h]
-            arrived(ref, first[1 + d])
-            send(ref, ref, first[4 + d], {"dp": h_peer})
-        prepare(0, 2)
-        arrived(wa.at[z, x, 1 - h], first[0])
-        for d in range(3):
-            arrived(wa.at[z, (x + 3 - d) % 4, 1 - h], first[4 + d])
         right = {"dp": at((z + 1) % 8, x, h, c)}
         left = {"dp": at((z + 7) % 8, x, h, c)}
 
@@ -285,31 +278,56 @@
             ref = slot_a(place(kind, s), q)
             send(ref, ref, hand_a[(kind, s, q)], other)
 
-        for kind, q in (("r", 0), ("l", 1), ("r", 1), ("l", 0)):
-            pass_on(kind, 1, q)
+        def hop(s, q):
+            for kind in ("r", "l"):
+                if (kind, s, q) in pass_a:
+                    arrived(slot_a(place(kind, s), q), pass_a[(kind, s, q)])
+                    if (kind, s + 1, q) in pass_a:
+                        pass_on(kind, s + 1, q)
+                    hand(kind, s, q)
+
+        def theirs(name):
+            for q in range(2):
+                arrived(wb.at[place_b[name], (h + q) % 2], hand_b[(name, q)])
+            multiply_b(place_b[name])
+
+        for d in range(3):
+            ref = wa.at[z, h, (x + 3 - d) % 4]
+            arrived(ref, first[1 + d])
+            send(ref, ref, first[4 + d], {"dp": h_peer})
+        pass_on("r", 1, 0)
+        pass_on("l", 1, 0)
         hand("r", 0, 0)
+        prepare(0, 3)
+        hop(1, 0)
+        arrived(wa.at[z, 1 - h, x], first[0])
+        for d in range(3):
+            arrived(wa.at[z, 1 - h, (x + 3 - d) % 4], first[4 + d])
+        pass_on("r", 1, 1)
+        pass_on("l", 1, 1)
         hand("r", 0, 1)
-        prepare(2, 8)
-        todo = [(z, 0), (z, 1)]
-        for s in range(1, 5):
-            ready = []
-            for kind, q in (("r", 0), ("l", 1), ("r", 1), ("l", 0)):
-                if (kind, s, q) not in pass_a:
-                    continue
-                arrived(slot_a(place(kind, s), q), pass_a[(kind, s, q)])
-                if (kind, s + 1, q) in pass_a:
-                    pass_on(kind, s + 1, q)
-                hand(kind, s, q)
-                ready.append((place(kind, s), q))
-            for zz, q in todo:
-                multiply_a(zz, 2 * q, 2)
-            todo = ready
-        for zz, q in todo:
-            multiply_a(zz, 2 * q, 2)
-        for n in ("own", "left", "right", "far"):
-            for q in range(2):
-                arrived(wb.at[place_b[n], q], hand_b[(n, q)])
-            multiply_b(place_b[n])
+        prepare(3, 5)
+        hop(2, 0)
+        prepare(5, 7)
+        hop(1, 1)
+        prepare(7, 8)
+        hop(3, 0)
+        multiply_a(z)
+        hop(2, 1)
+        multiply_a(place("r", 1))
+        multiply_a(place("l", 1))
+        theirs("own")
+        hop(4, 0)
+        hop(3, 1)
+        multiply_a(place("r", 2))
+        multiply_a(place("l", 2))
+        theirs("left")
+        theirs("right")
+        hop(4, 1)
+        multiply_a(place("r", 3))
+        multiply_a(place("l", 3))
+        theirs("far")
+        multiply_a(place("r", 4))
         for copy in sent[base:]:
             copy.wait_send()
         del sent[base:]
@@ -325,42 +343,49 @@
             ref = wb.at[x, h, (z + 7 - d) % 8]
             arrived(ref, first[1 + d])
             send(ref, ref, first[8 + d], {"dp": h_peer})
-        prepare(0, 3)
+        right = {"dp": x_peers[0]}
+        left = {"dp": x_peers[2]}
+        xl, xr = place_b["left"], place_b["right"]
+
+        def slot_b(xx, q):
+            return wb.at[xx, (h + q) % 2]
+
+        def spread_own(q):
+            send(slot_b(x, q), slot_b(x, q), pass_b["r" + str(q)], right)
+            send(slot_b(x, q), slot_b(x, q), pass_b["l" + str(q)], left)
+            send(slot_b(x, q), slot_b(x, q), hand_b[("own", q)], other)
+
+        def got_b(xx, q, name, to, sem, target):
+            arrived(slot_b(xx, q), pass_b[name])
+            if target is not None:
+                send(slot_b(xx, q), slot_b(xx, q), pass_b[sem], target)
+            send(slot_b(xx, q), slot_b(xx, q), hand_b[(to, q)], other)
+
+        spread_own(0)
+        prepare(0, 2)
+        got_b(xl, 0, "r0", "left", "far0", right)
+        got_b(xr, 0, "l0", "right", None, None)
+        prepare(2, 3)
         arrived(wb.at[x, 1 - h, z], first[0])
         for d in range(7):
             arrived(wb.at[x, 1 - h, (z + 7 - d) % 8], first[8 + d])
-        right = {"dp": x_peers[0]}
-        left = {"dp": x_peers[2]}
-        for name, q, target in (("r0", 0, right), ("l1", 1, left), ("r1", 1, right), ("l0", 0, left)):
-            send(wb.at[x, q], wb.at[x, q], pass_b[name], target)
-        for q in range(2):
-            send(wb.at[x, q], wb.at[x, q], hand_b[("own", q)], other)
+        spread_own(1)
+        got_b(far, 0, "far0", "far", None, None)
         prepare(3, 8)
-        xl, xr = place_b["left"], place_b["right"]
-        arrived(wb.at[xl, 0], pass_b["r0"])
-        send(wb.at[xl, 0], wb.at[xl, 0], pass_b["far0"], right)
-        send(wb.at[xl, 0], wb.at[xl, 0], hand_b[("left", 0)], other)
-        arrived(wb.at[xr, 1], pass_b["l1"])
-        send(wb.at[xr, 1], wb.at[xr, 1], pass_b["far1"], left)
-        send(wb.at[xr, 1], wb.at[xr, 1], hand_b[("right", 1)], other)
+        got_b(xr, 1, "l1", "right", "far1", left)
+        got_b(xl, 1, "r1", "left", None, None)
         multiply_b(x)
-        arrived(wb.at[xl, 1], pass_b["r1"])
-        send(wb.at[xl, 1], wb.at[xl, 1], hand_b[("left", 1)], other)
-        arrived(wb.at[xr, 0], pass_b["l0"])
-        send(wb.at[xr, 0], wb.at[xr, 0], hand_b[("right", 0)], other)
         multiply_b(xl)
-        arrived(wb.at[far, 0], pass_b["far0"])
-        send(wb.at[far, 0], wb.at[far, 0], hand_b[("far", 0)], other)
-        arrived(wb.at[far, 1], pass_b["far1"])
-        send(wb.at[far, 1], wb.at[far, 1], hand_b[("far", 1)], other)
         multiply_b(xr)
+        got_b(far, 1, "far1", "far", None, None)
         multiply_b(far)
         for s in range(5):
-            for kind, q in (("r", 0), ("l", 1), ("r", 1), ("l", 0)):
-                if (kind, s, q) not in hand_a:
-                    continue
-                arrived(slot_a(place(kind, s), q), hand_a[(kind, s, q)])
-                multiply_a(place(kind, s), 2 * q, 2)
+            for kind, q in (("r", 0), ("l", 0), ("r", 1), ("l", 1)):
+                if (kind, s, q) in hand_a:
+                    arrived(slot_a(place(kind, s), q), hand_a[(kind, s, q)])
+            multiply_a(place("r", s))
+            if 0 < s < 4:
+                multiply_a(place("l", s))
         for copy in sent[base:]:
             copy.wait_send()
         del sent[base:]
@@ -517,15 +542,21 @@
     home = z // 2
     order = [home, (home + 4 + swing) % 4, (home + 4 - swing) % 4, (home + 2) % 4]
     spans = [pl.ds(pl.multiple_of(128 * i, 128), 128) for i in order]
-    here = iota((128, 640), 0)
-    there = iota((128, 640), 1)
+    shift = jnp.where(iota((128, 128), 0) == iota((128, 128), 1), damping, 0.0)
+    spans.append(pl.ds(512, 128))
+
+    def exact(u, v):
+        return jnp.dot(u, v, precision=HIGH, preferred_element_type=F32)
 
     def eliminate(t):
-        a[t] = kin[spans[t], :] + jnp.where(there == here + 128 * order[t], damping, 0.0)
+        for m in range(5):
+            a[t, m] = kin[spans[t], spans[m]] + shift if m == t else kin[spans[t], spans[m]]
         for n in range(t):
-            a[t] = a[t] - jnp.dot(a[t, :, spans[n]], a[n], precision=HIGH, preferred_element_type=F32)
-        inv = invert(a[t, :, spans[t]], lambda: take_hop(t + 2))
-        a[t] = jnp.dot(inv, a[t], precision=HIGH, preferred_element_type=F32)
+            for m in range(n + 1, 5):
+                a[t, m] = a[t, m] - exact(a[t, n], a[n, m])
+        inv = invert(a[t, t], lambda: take_hop(t + 2))
+        for m in range(t + 1, 5):
+            a[t, m] = exact(inv, a[t, m])
 
     for kind, q in (("r", 0), ("l", 1), ("r", 1), ("l", 0)):
         pass_rows(kind, 1, q)
@@ -543,19 +574,14 @@
             arrived(rows_at(1 - c, place(kind, s), q), ring[(kind, s, q)][1])
         eliminate(s - 1)
 
-    def apply(left_rows, n, value):
-        return jnp.dot(left_rows(spans[n]), value, precision=HIGH, preferred_element_type=F32)
-
-    x3 = a[3, :, 512:640]
-    x2 = a[2, :, 512:640] - apply(lambda at_: a[2, :, at_], 3, x3)
-    x1 = a[1, :, 512:640] - apply(lambda at_: a[1, :, at_], 3, x3) - apply(lambda at_: a[1, :, at_], 2, x2)
+    x3 = a[3, 4]
+    x2 = a[2, 4] - exact(a[2, 3], x3)
+    x1 = a[1, 4] - exact(a[1, 3], x3) - exact(a[1, 2], x2)
     pick = jnp.where(iota((8, 128), 1) == (me * 4 - 128 * home) + iota((8, 128), 0), 1.0, 0.0).astype(F32)
-    own_x = jnp.dot(pick, a[0, :, 512:640], precision=HIGH, preferred_element_type=F32)
+    own_x = exact(pick, a[0, 4])
     for n, value in ((3, x3), (2, x2), (1, x1)):
-        coef = jnp.dot(pick, a[0, :, spans[n]], precision=HIGH, preferred_element_type=F32)
-        own_x = own_x - jnp.dot(coef, value, precision=HIGH, preferred_element_type=F32)
+        own_x = own_x - exact(exact(pick, a[0, n]), value)
     own_x = own_x[0:4]
-    load_x.wait()
     lanes = iota((4, 128), 1)
     spot = iota((4, 8), 1)
     out = jnp.zeros((4, 8), F32)
@@ -577,7 +603,7 @@
         out_specs=(vmem, vmem),
         scratch_shapes=[
             pltpu.VMEM((512, 640), F32),
-            pltpu.VMEM((4, 128, 640), F32),
+            pltpu.VMEM((4, 5, 128, 128), F32),
             pltpu.VMEM((8, 8, 128), F32),
             pltpu.VMEM((4, 8, 128), F32),
             pltpu.VMEM((4, 8), jnp.int32),
@@ -588,7 +614,7 @@
             pltpu.VMEM(qry.shape, BF16),
             pltpu.SMEM((1, 4), jnp.int32),
             pltpu.VMEM((2, 8, 4, 256, 256), BF16),
-            pltpu.VMEM((8, 4, 2, 64, 128), BF16),
+            pltpu.VMEM((8, 2, 4, 64, 128), BF16),
             pltpu.VMEM((4, 2, 8, 64, 128), BF16),
             pltpu.VMEM((2, 4, 2, 128, 128), BF16),
             pltpu.VMEM((9, 128, 128), BF16),

time: 98.2 us -> 95.3 us (0.970)
  Pallas kernels: 96.1 us -> 93.3 us
    pallas_call x1, Pallas kernels: 96.1 us -> 93.3 us  [run_front(): pl.pallas_call(front, out_shape=(jax.ShapeDtypeStruct((4, 4096), BF16), j...]
where the time goes in v4:
time: 95.3 us; the launch traced here: 95.1 us
  Pallas kernels  93.3 us (98%)
  local copies, waits for them, and re-layouts  1.19 us (1%)
    pallas_call x1, Pallas kernels, run_front(): pl.pallas_call(front, out_shape=(jax.ShapeDtypeStruct((4, 4096), BF16), j...  93.3 us

profile of v4, /device:TPU:1, one launch (start us, length us, event | category | flops | bytes accessed | tf_op | source)
XLA Modules:
  0.0 95.1 jit_solution(7045130769949496239)
XLA Ops:
  0.6 93.3 %front.1 = (bf16[4,4096]{1,0:T(4,128)(2,1)S(1)}, f32[4,8]{1,0:T(4,128)S(1)}) custom-call(bf16[128,9728]{1,0:T(8,128)(2,1)} %bitcast.9, bf16[128,3584]{1,0:T(8,128)(2,1)} %bitcast.10, bf16[64,76]{1,0:T(8,128)(2,1)} %bitcast.12, bf16[28,64]{1,0:T(8,128)(2,1)} %bitcast.13, bf16[64,4096]{1,0:T(8,128)(2,1)} %bitcast.11, s32[1,4]{1,0:T(1,128)} %lens_hbm.1, ...), custom_call_target="tpu_custom_call" | custom-call | tf_op jit(solution)/shard_map/front/pallas_call | solution.py:599
  93.9 0.6 copy.11
  94.5 0.6 copy.12

commit v5 on v4

--- a/solution.py
+++ b/solution.py
@@ -172,8 +172,11 @@
     def _():
         wb[x, h, z] = own
 
+    def loaded():
+        for load in (load_q, load_l, load_x, load_a, load_g):
+            load.wait()
+
     def tables():
-        load_q.wait()
         q_row = iota((8, 64), 0)
         q_col = iota((8, 64), 1)
         low = onehot((q_row < 4) & (q_col == 4 * b + q_row))
@@ -186,10 +189,6 @@
         col = iota((128, 512), 1)
         for j in range(16):
             perm[pl.ds(128 * j, 128), :] = onehot(col == ((lane // 4) % 8) * 64 + j * 4 + lane % 4)
-        load_l.wait()
-        load_x.wait()
-        load_a.wait()
-        load_g.wait()
 
     acc[...] = jnp.zeros_like(acc)
 
@@ -266,7 +265,7 @@
         ref = wa.at[z, h, x]
         for i, peer in enumerate([h_peer] + x_peers):
             send(ref, ref, first[i], {"dp": peer})
-        tables()
+        loaded()
         right = {"dp": at((z + 1) % 8, x, h, c)}
         left = {"dp": at((z + 7) % 8, x, h, c)}
 
@@ -338,7 +337,7 @@
         ref = wb.at[x, h, z]
         for i, peer in enumerate([h_peer] + z_peers):
             send(ref, ref, first[i], {"dp": peer})
-        tables()
+        loaded()
         for d in (0, 6, 1, 5, 2, 4, 3):
             ref = wb.at[x, h, (z + 7 - d) % 8]
             arrived(ref, first[1 + d])
@@ -421,6 +420,7 @@
     s_z = [take() for _ in range(7)]
     for d in range(7):
         send(scol.at[z], scol.at[z], s_z[d], {"dp": z_peers[d]})
+    tables()
     arrived(srow.at[c, x, 1 - h], s_h)
     s_x = [take() for _ in range(3)]
     s_c = [take() for _ in range(4)]

time: 95.3 us -> 95.8 us (level)
  no operation moved by 1% of the time
where the time goes in v5:
time: 95.8 us; the launch traced here: 95.6 us
  Pallas kernels  93.8 us (98%)
  local copies, waits for them, and re-layouts  1.19 us (1%)
    pallas_call x1, Pallas kernels, run_front(): pl.pallas_call(front, out_shape=(jax.ShapeDtypeStruct((4, 4096), BF16), j...  93.8 us

profile of v5, /device:TPU:1, one launch (start us, length us, event | category | flops | bytes accessed | tf_op | source)
XLA Modules:
  0.0 95.6 jit_solution(15314590957657471245)
XLA Ops:
  0.6 93.8 %front.1 = (bf16[4,4096]{1,0:T(4,128)(2,1)S(1)}, f32[4,8]{1,0:T(4,128)S(1)}) custom-call(bf16[128,9728]{1,0:T(8,128)(2,1)} %bitcast.9, bf16[128,3584]{1,0:T(8,128)(2,1)} %bitcast.10, bf16[64,76]{1,0:T(8,128)(2,1)} %bitcast.12, bf16[28,64]{1,0:T(8,128)(2,1)} %bitcast.13, bf16[64,4096]{1,0:T(8,128)(2,1)} %bitcast.11, s32[1,4]{1,0:T(1,128)} %lens_hbm.1, ...), custom_call_target="tpu_custom_call" | custom-call | tf_op jit(solution)/shard_map/front/pallas_call | solution.py:599
  94.4 0.6 copy.11
  95.0 0.6 copy.12
